TPU v7x, 128 devices: a whole 4x4x4 slice. The times are simulated.
128 devices in a mesh: scen: 4 (over z_hi, core), trade: 32 (over z_lo, x, y).
Axes of the slice: x: 4, y: 4, z: 4 (z_hi: 2, z_lo: 2; z = z_hi * 2 + z_lo), core: 2. Of those that a mesh axis runs over, the one named last changes fastest.
Arguments:
- normal_draws: bfloat16 [2, 2048, 4096], P(None, 'scen', 'trade'), may hold values from -6 to 6
- covariance_root: bfloat16 [4096, 4096], P('trade'), as said below
- mean_pullback: float32 [4096], replicated, may hold values from 0.3 to 0.97
- sensitivity_tensor: bfloat16 [4096, 65536], P(None, 'trade'), may hold values from -0.09375 to 0.09375
- moneyness_shift: float32 [65536], P('trade'), may hold values from -5 to 5
- signed_principal: float32 [65536], P('trade'), may hold values from -1 to 1
- deal_agreement_group: int32 [65536], P('trade'), may hold values from 0 to 511
- active_position_number: int32 [32], P('trade'), may hold values from 512 to 2048, as said below
Outputs:
- exposure: float32 [2, 2048, 512], P(None, 'scen', 'trade')
- expected_exposure: float32 [2, 512], P(None, 'trade')
Inputs may be any that keep to these rules, and one draw needn't show every extreme that they name: Each trade shard's first active_position_number slots hold trades, the rest are empty; some shard holds 2048 live trades in every draw. `covariance_root`: upper triangular with a positive diagonal.
All inputs are finite; a program needn't handle non-finite values.
Results may differ from a plain program's by a relative error of at most 0.0034.
Values may be sent and summed in bfloat16 or wider, within the bound.
A program may use at most 128 MiB of HBM per device.

v0:
```python
import jax
import jax.numpy as jnp
from jax import lax
from jax.sharding import PartitionSpec as P

SETS_DEV = 16


def on_device(
    normal_draws,
    covariance_root,
    mean_pullback,
    sensitivity_tensor,
    moneyness_shift,
    signed_principal,
    deal_agreement_group,
    active_position_number,
):
    date_count = normal_draws.shape[0]
    group_rows = normal_draws.shape[1]
    factor_width = covariance_root.shape[1]
    trade_parts = lax.axis_size("trade")
    position_overall_sum = sensitivity_tensor.shape[1]
    tile_fields = min(256, position_overall_sum)
    set_total = SETS_DEV * trade_parts
    live_count = active_position_number[0]
    weight = jnp.where(
        jnp.arange(position_overall_sum, dtype=jnp.int32) < live_count,
        signed_principal,
        jnp.zeros_like(signed_principal),
    )
    block_total = (live_count + tile_fields - 1) // tile_fields
    labels = jnp.arange(set_total, dtype=jnp.int32)
    date_groups = [(date_index, 1) for date_index in range(date_count)]
    factor_state = jnp.zeros((group_rows, factor_width), jnp.float32)
    exposures = []
    for opening, number in date_groups:
        partials = jnp.dot(
            normal_draws[opening], covariance_root, preferred_element_type=jnp.float32
        )
        shock_sums = lax.psum(partials, "trade")
        factor_state = mean_pullback * factor_state + shock_sums
        level_list = [factor_state.astype(jnp.bfloat16)]
        levels = jnp.stack(level_list, 1)[:, 0, :]

        def block_step(block_index, running):
            position_start = block_index * tile_fields
            field_indices = lax.dynamic_slice_in_dim(
                sensitivity_tensor, position_start, tile_fields, 1
            )
            moneyness = jnp.dot(levels, field_indices, preferred_element_type=jnp.float32)
            moneyness = moneyness + lax.dynamic_slice_in_dim(
                moneyness_shift, position_start, tile_fields, 0
            )
            scaled = lax.dynamic_slice_in_dim(weight, position_start, tile_fields, 0)
            values = (scaled * jax.nn.softplus(moneyness)).astype(jnp.bfloat16)
            set_ids = lax.dynamic_slice_in_dim(deal_agreement_group, position_start, tile_fields, 0)
            member = (set_ids[:, None] == labels[None, :]).astype(jnp.bfloat16)
            return running + jnp.dot(values, member, preferred_element_type=jnp.float32)

        net_terms = jnp.stack(
            [
                lax.fori_loop(
                    0, block_total, block_step, jnp.zeros((levels.shape[0], set_total), jnp.float32)
                )
            ],
            0,
        )
        owned_net = lax.psum_scatter(net_terms, "trade", scatter_dimension=2, tiled=True)
        exposures.append(jnp.maximum(owned_net, 0.0))
    exposure = jnp.concatenate(exposures, 0)
    exposure_mean = lax.psum(jnp.sum(exposure, axis=1), "scen") / (
        group_rows * lax.axis_size("scen")
    )
    return (exposure, exposure_mean)


def solution(mesh):
    in_specs = (
        P(None, "scen", "trade"),
        P("trade", None),
        P(),
        P(None, "trade"),
        P("trade"),
        P("trade"),
        P("trade"),
        P("trade"),
    )
    out_specs = (P(None, "scen", "trade"), P(None, "trade"))
    return jax.shard_map(
        on_device, mesh=mesh, in_specs=in_specs, out_specs=out_specs, check_vma=False
    )
```

profile of v0, /device:TPU:1, one launch (start us, length us, event | category | flops | bytes accessed | tf_op | source)
XLA Modules:
  0.0 810.8 jit_solution(17490233923289316303)
XLA Ops:
  7.2 1.2 copy-done
  8.4 5.4 fusion.46
  13.8 4.4 fusion.48
  19.0 397.0 %all-reduce.3.cloned.1.call-done = (f32[512,4096]{1,0:T(8,128)}, f32[512,4096]{1,0:T(8,128)}) async-done(((f32[512,4096]{1,0:T(8,128)}, f32[512,4096]{1,0:T(8,128)}), (f32[512,4096]{1,0:T(8,128)}, f32[512,4096]{1,0:T(8,128)})) %all-reduce.3.cloned.1.call-update) | async-done | bytes 16777232 | tf_op jit(solution)/shard_map/psum | solution.py:41
  416.0 9.5 %add_convert_fusion.1 = (bf16[512,4096]{1,0:T(8,128)(2,1)}, bf16[512,4096]{1,0:T(8,128)(2,1)}) fusion(f32[512,4096]{1,0:T(8,128)} %get-tuple-element.171, f32[4096]{0:T(1024)S(1)} %broadcast_multiply_fusion, f32[512,4096]{1,0:T(8,128)} %get-tuple-element.170, f32[4096]{0:T(1024)S(1)} %copy-done.2), kind=kLoop, calls=%fused_computation.33 | loop fusion | flops 10485760 | bytes 25198592 | tf_op jit(solution)/shard_map/convert_element_type | solution.py:43
  425.5 51.4 %while.22 = (s32[]{:T(128)}, f32[512,512]{1,0:T(8,128)S(1)}, s32[]{:T(128)}, f32[2048]{0:T(1024)S(1)}, bf16[4096,2048]{1,0:T(8,128)(2,1)}, /*index=5*/bf16[512,4...) while((s32[]{:T(128)}, f32[512,512]{1,0:T(8,128)S(1)}, ...), condition=%wide.region_2.3_spmd.clone, body=%wide.region_1.2_spmd.clone.sunk | while | flops 1209532416 | bytes 8398003 | solution.py:63
  425.6 0.8 dynamic_slice.61
  427.2 4.8 convolution_add_fusion.4
  432.0 0.8 dynamic_slice.61
  433.6 4.8 convolution_add_fusion.4
  438.4 0.8 dynamic_slice.61
  440.0 4.8 convolution_add_fusion.4
  444.8 0.8 dynamic_slice.61
  446.4 4.8 convolution_add_fusion.4
  451.3 0.8 dynamic_slice.61
  452.9 4.8 convolution_add_fusion.4
  457.7 0.8 dynamic_slice.61
  459.3 4.8 convolution_add_fusion.4
  464.1 0.8 dynamic_slice.61
  465.7 4.8 convolution_add_fusion.4
  470.5 0.8 dynamic_slice.61
  472.1 4.8 convolution_add_fusion.4
  477.0 1.3 copy.10
  478.5 51.5 %while.23 = (s32[]{:T(128)}, f32[512,512]{1,0:T(8,128)S(1)}, s32[]{:T(128)}, f32[2048]{0:T(1024)S(1)}, bf16[4096,2048]{1,0:T(8,128)(2,1)}, /*index=5*/bf16[512,4...) while((s32[]{:T(128)}, f32[512,512]{1,0:T(8,128)S(1)}, ...), condition=%wide.region_6.7_spmd.clone, body=%wide.region_5.6_spmd.clone.sunk | while | flops 1209532416 | bytes 8398003 | solution.py:63
  478.5 0.8 dynamic_slice.65
  480.1 4.8 convolution_add_fusion.5
  484.9 0.8 dynamic_slice.65
  486.5 4.8 convolution_add_fusion.5
  491.3 0.8 dynamic_slice.65
  492.1 0.8 dynamic_slice.66
  492.9 4.8 convolution_add_fusion.5
  497.8 0.8 dynamic_slice.65
  498.5 0.8 dynamic_slice.66
  499.4 4.8 convolution_add_fusion.5
  504.2 0.8 dynamic_slice.65
  505.8 4.8 convolution_add_fusion.5
  510.6 0.8 dynamic_slice.65
  512.2 4.8 convolution_add_fusion.5
  517.1 0.8 dynamic_slice.65
  518.7 4.8 convolution_add_fusion.5
  523.5 0.8 dynamic_slice.65
  525.1 4.8 convolution_add_fusion.5
  529.9 1.3 copy.11
  531.3 79.5 %reduce-scatter.3.cloned.1.call-done = f32[1,512,16]{1,2,0:T(8,128)} async-done(((f32[1,512,512]{1,2,0:T(8,128)}), f32[1,512,16]{1,2,0:T(8,128)}) %reduce-scatter.3.cloned.1.call-update) | async-done | bytes 32784 | tf_op jit(solution)/shard_map/reduce_scatter | solution.py:69
  610.8 0.8 broadcast_maximum_fusion.1
  611.6 159.2 %reduce-scatter.5.cloned.1.call-done = f32[1,512,16]{1,2,0:T(8,128)} async-done(((f32[1,512,512]{1,2,0:T(8,128)}), f32[1,512,16]{1,2,0:T(8,128)}) %reduce-scatter.5.cloned.1.call-update) | async-done | bytes 32784 | tf_op jit(solution)/shard_map/reduce_scatter | solution.py:69
  770.8 0.8 broadcast_maximum_fusion
  772.2 31.6 %psum.23 = f32[2,16]{1,0:T(2,128)S(1)} all-reduce(f32[2,16]{1,0:T(2,128)S(1)} %get-tuple-element.172), channel_id=1, replica_groups=mesh['scen'=4,'trade'=32] {'scen'}, use_global_device_ids=true, to_apply=%region_9.10 | all-reduce | flops 32 | bytes 256 | tf_op jit(solution)/shard_map/psum | solution.py:72
  (49 shorter events, 13.4 us)
Async XLA Ops:
  7.2 1.2 copy-start
  7.2 6.6 copy-start.1
  7.2 408.8 %all-reduce.3.cloned.1.call-start = ((), (), s32[]{:S(2)}) async-start(), calls=%async_computation.4 | async-start | bytes 33554432 | tf_op jit(solution)/shard_map/psum | solution.py:41
  18.2 0.7 copy-start.3
  18.2 0.8 copy-start.2
  18.2 592.6 %reduce-scatter.3.cloned.1.call-start = ((), (), s32[]{:S(2)}) async-start(), calls=%async_computation.2 | async-start | bytes 1081344 | tf_op jit(solution)/shard_map/reduce_scatter | solution.py:69
  478.3 292.5 %reduce-scatter.5.cloned.1.call-start = ((), (), s32[]{:S(2)}) async-start(), calls=%async_computation.3 | async-start | bytes 1081344 | tf_op jit(solution)/shard_map/reduce_scatter | solution.py:69
Sparse Core Ops, SparseCore 0:
  18.4 397.5 all-reduce.2
  478.4 132.3 reduce-scatter.2
  613.3 157.4 reduce-scatter.4
where the time goes:
time: 813 us; the launch traced here: 811 us
  waiting for transfers between devices  636 us (78%)
  matrix products  86.6 us (11%)
  blocking collectives  31.6 us (4%)
  local copies, waits for them, and re-layouts  29.6 us (4%)
  between operations  14.5 us (2%)
  other arithmetic  12.2 us (2%)
    psum x1, waiting for transfers between devices, on_device(): shock_sums = lax.psum(partials, 'trade')  397 us
    reduce_scatter x2, waiting for transfers between devices, on_device(): lax.psum_scatter(net_terms, 'trade', scatter_dimension=2, tiled=True)  239 us
    dot_general x16, matrix products, block_step(): return running + jnp.dot(values, member, preferred_element_type=jnp.float32)  76.8 us
    psum x1, blocking collectives, on_device(): lax.psum(jnp.sum(exposure, axis=1), 'scen')  31.6 us
  transfers between devices with their start and end apart: 3, of which 3 were waited for; matrix products, arithmetic and copies ran while one was open for 7% of the time, Pallas kernels for 0%

commit v1 on v0

v1 whole, which is shorter than its diff:
```python
import functools
import jax
import jax.numpy as jnp
from jax import lax
from jax.experimental import pallas as pl
from jax.experimental.pallas import tpu as pltpu
from jax.sharding import PartitionSpec as P

F32, BF16 = jnp.float32, jnp.bfloat16
SETS_DEV = 16
NZ, NX, NY = 2, 4, 4
N_TRADE = NZ * NX * NY
CHUNKS = 4
COLS = 4
ROWS = 64
LANES = 128
TILE = 256
PARTS = (
    ((0, 3), (0, 32), ("z", "y", "x")),
    ((0, 3), (32, 32), ("z", "x", "y")),
    ((3, 1), (0, 64), ("x", "y", "z")),
)
STEPS = 5


def trade_place():
    me = lax.axis_index("trade")
    return {"z": me // (NX * NY), "x": (me // NY) % NX, "y": me % NY}


def trade_index(place):
    return (place["z"] * NX + place["x"]) * NY + place["y"]


def moved(place, axis, by):
    size = {"z": NZ, "x": NX, "y": NY}[axis]
    return dict(place, **{axis: (place[axis] + by) % size})


def part_steps(place, order):
    have = dict(place)
    steps = []
    for axis in order:
        if axis == "z":
            steps.append(
                (
                    [(dict(have), None, moved(place, "z", 1))],
                    [(dict(have, z=1 - place["z"]), None)],
                )
            )
        else:
            right, left = moved(place, axis, 1), moved(place, axis, 3)
            far = moved(place, axis, 2)
            at = lambda where: dict(have, **{axis: where[axis]})
            steps.append(
                (
                    [(at(place), None, right), (at(place), None, left)],
                    [(at(left), None), (at(right), None)],
                )
            )
            steps.append(
                (
                    [(at(left), 0, right), (at(right), 1, left)],
                    [(at(far), 0), (at(far), 1)],
                )
            )
        have[axis] = None
    return steps


def softplus(a):
    return jnp.maximum(a, 0.0) + jnp.log1p(jnp.exp(-jnp.abs(a)))


def value_kernel(
    lev_hbm, sens_hbm, shift_ref, principal_ref, group_ref, live_ref, out_ref,
    book, sens, member, weight, net, net_out, net_in,
    send_sems, recv_sems, own_sem, sens_sem, net_send_sem, net_recv_sems,
):
    place = trade_place()
    me = trade_index(place)
    positions = sens.shape[1]
    sets = member.shape[0]

    fetch = pltpu.make_async_copy(sens_hbm, sens, sens_sem)
    fetch.start()
    own = pltpu.make_async_copy(
        lev_hbm, book.at[:, place["z"], place["x"], :, place["y"]], own_sem
    )
    own.start()

    barrier = pltpu.get_barrier_semaphore()

    @pl.loop(1, N_TRADE)
    def _(step):
        pl.semaphore_signal(
            barrier, inc=1, device_id={"trade": (me + step) % N_TRADE},
            device_id_type=pl.DeviceIdType.MESH,
        )

    pl.semaphore_wait(barrier, N_TRADE - 1)
    own.wait()

    plans = [part_steps(place, order) for _, _, order in PARTS]

    def view(part, chunk, coords, half):
        (col, cols), (row, rows), _ = PARTS[part]
        if half is not None:
            rows = rows // 2
            row = row + half * rows
        pick = [slice(None) if coords[a] is None else coords[a] for a in "zxy"]
        return book.at[chunk, pick[0], pick[1], pl.ds(col, cols), pick[2], pl.ds(row, rows), :]

    def descriptors(part, step, chunk, kind):
        sends, recvs = plans[part][step]
        for way in range(len(sends)):
            if kind == "send":
                coords, half, target = sends[way]
            else:
                coords, half = recvs[way]
                target = place
            ref = view(part, chunk, coords, half)
            yield pltpu.make_async_remote_copy(
                src_ref=ref, dst_ref=ref,
                send_sem=send_sems.at[chunk, part, step, way],
                recv_sem=recv_sems.at[chunk, part, step, way],
                device_id={"trade": trade_index(target)},
                device_id_type=pl.DeviceIdType.MESH,
            )

    def start(step, chunk):
        for part in range(len(PARTS)):
            for copy in descriptors(part, step, chunk, "send"):
                copy.start()

    def arrived(step, chunk):
        for part in range(len(PARTS)):
            for copy in descriptors(part, step, chunk, "recv"):
                copy.wait_recv()

    @pl.loop(0, CHUNKS)
    def _(chunk):
        start(0, chunk)

    weight[...] = jnp.where(
        lax.broadcasted_iota(jnp.int32, (1, positions), 1) < live_ref[...],
        principal_ref[...], 0.0,
    )
    @pl.loop(0, positions // TILE)
    def _(tile):
        at = pl.ds(pl.multiple_of(tile * TILE, TILE), TILE)
        labels = lax.broadcasted_iota(jnp.int32, (sets, TILE), 0)
        member[:, at] = (labels == group_ref[:, at]).astype(F32).astype(BF16)

    for step in (1, 2):
        @pl.loop(0, CHUNKS)
        def _(chunk, step=step):
            arrived(step - 1, chunk)
            start(step, chunk)

    fetch.wait()

    def net_copy(chunk, target):
        return pltpu.make_async_remote_copy(
            src_ref=net_out.at[chunk, target], dst_ref=net_in.at[chunk, me],
            send_sem=net_send_sem, recv_sem=net_recv_sems.at[chunk],
            device_id={"trade": target}, device_id_type=pl.DeviceIdType.MESH,
        )

    def compute(chunk):
        net[...] = jnp.zeros_like(net)
        levels = jnp.concatenate(
            [
                book[chunk, z, x, col].reshape(NY * ROWS, LANES)
                for z in range(NZ) for x in range(NX) for col in range(COLS)
            ],
            axis=1,
        )

        @pl.loop(0, positions // TILE)
        def _(tile):
            at = pl.ds(pl.multiple_of(tile * TILE, TILE), TILE)
            moneyness = jnp.dot(levels, sens[:, at], preferred_element_type=F32)
            values = weight[:, at] * softplus(moneyness + shift_ref[:, at])
            net[...] += lax.dot_general(
                member[:, at], values.astype(BF16), (((1,), (1,)), ((), ())),
                preferred_element_type=F32,
            )

        net_out[chunk] = net[...].astype(BF16).reshape(N_TRADE, SETS_DEV, NY * ROWS)

        @pl.loop(1, N_TRADE)
        def _(step):
            net_copy(chunk, (me + step) % N_TRADE).start()

        net_in[chunk, me] = net_out[chunk, me]

    @pl.loop(0, CHUNKS + 2)
    def _(tick):
        @pl.when(tick < CHUNKS)
        def _():
            arrived(2, tick)
            start(3, tick)

        @pl.when(jnp.logical_and(tick >= 1, tick < CHUNKS + 1))
        def _():
            arrived(3, tick - 1)
            start(4, tick - 1)

        @pl.when(tick >= 2)
        def _():
            arrived(4, tick - 2)
            compute(tick - 2)

    @pl.loop(0, CHUNKS)
    def _(chunk):
        for part in range(len(PARTS)):
            for step in range(STEPS):
                for copy in descriptors(part, step, chunk, "send"):
                    copy.wait_send()

        whole = pltpu.make_async_remote_copy(
            src_ref=net_out.at[chunk, pl.ds(0, N_TRADE - 1)],
            dst_ref=net_in.at[chunk, pl.ds(0, N_TRADE - 1)],
            send_sem=net_send_sem, recv_sem=net_recv_sems.at[chunk],
            device_id={"trade": me}, device_id_type=pl.DeviceIdType.MESH,
        )
        whole.wait_send()
        whole.wait_recv()
        total = jnp.zeros((SETS_DEV, NY * ROWS), F32)
        for sender in range(N_TRADE):
            total = total + net_in[chunk, sender].astype(F32)
        out_ref[chunk] = jnp.maximum(total, 0.0)


def values_and_nets(levels, sensitivity, shift, principal, group, live):
    positions = sensitivity.shape[1]
    sets = SETS_DEV * N_TRADE
    vmem = pl.BlockSpec(memory_space=pltpu.VMEM)
    hbm = pl.BlockSpec(memory_space=pl.ANY)
    return pl.pallas_call(
        value_kernel,
        out_shape=jax.ShapeDtypeStruct((CHUNKS, SETS_DEV, NY * ROWS), F32),
        in_specs=[hbm, hbm, vmem, vmem, vmem, vmem],
        out_specs=vmem,
        scratch_shapes=[
            pltpu.VMEM((CHUNKS, NZ, NX, COLS, NY, ROWS, LANES), BF16),
            pltpu.VMEM(sensitivity.shape, BF16),
            pltpu.VMEM((sets, positions), BF16),
            pltpu.VMEM((1, positions), F32),
            pltpu.VMEM((sets, NY * ROWS), F32),
            pltpu.VMEM((CHUNKS, N_TRADE, SETS_DEV, NY * ROWS), BF16),
            pltpu.VMEM((CHUNKS, N_TRADE, SETS_DEV, NY * ROWS), BF16),
            pltpu.SemaphoreType.DMA((CHUNKS, len(PARTS), STEPS, 2)),
            pltpu.SemaphoreType.DMA((CHUNKS, len(PARTS), STEPS, 2)),
            pltpu.SemaphoreType.DMA,
            pltpu.SemaphoreType.DMA,
            pltpu.SemaphoreType.DMA,
            pltpu.SemaphoreType.DMA((CHUNKS,)),
        ],
        compiler_params=pltpu.CompilerParams(
            collective_id=1, has_side_effects=True, vmem_limit_bytes=58 * 2**20
        ),
        cost_estimate=pl.CostEstimate(
            flops=2 * 1024 * positions * (4096 + sets), bytes_accessed=17 << 20, transcendentals=0
        ),
        name="value_nets",
    )(
        levels, sensitivity, shift.reshape(1, -1), principal.reshape(1, -1),
        group.reshape(1, -1), live.reshape(1, 1),
    )


def on_device(
    normal_draws, covariance_root, mean_pullback, sensitivity_tensor,
    moneyness_shift, signed_principal, deal_agreement_group, active_position_number,
):
    dates, scen = normal_draws.shape[:2]
    span = scen // NY // CHUNKS
    partial = jnp.dot(normal_draws, covariance_root, preferred_element_type=F32)
    partial = partial.reshape(dates, NY, CHUNKS, span, NZ * NX, COLS, LANES)
    partial = partial.transpose(4, 1, 2, 5, 0, 3, 6)
    partial = partial.reshape(N_TRADE, CHUNKS, COLS, dates, span, LANES)
    shocks = lax.psum_scatter(partial, "trade", scatter_dimension=0, tiled=False)
    zx = lax.axis_index("trade") // NY
    pull = lax.dynamic_index_in_dim(mean_pullback.reshape(NZ * NX, 1, COLS, 1, LANES), zx, 0, False)
    state = shocks[:, :, 0]
    states = [state]
    for date in range(1, dates):
        state = pull * state + shocks[:, :, date]
        states.append(state)
    levels = jnp.stack(states, 2).astype(BF16).reshape(CHUNKS, COLS, ROWS, LANES)
    nets = values_and_nets(
        levels, sensitivity_tensor, moneyness_shift, signed_principal,
        deal_agreement_group, active_position_number,
    )
    nets = nets.reshape(CHUNKS, SETS_DEV, NY, dates, span)
    exposure = nets.transpose(3, 2, 0, 4, 1).reshape(dates, scen, SETS_DEV)
    mean = lax.psum(jnp.sum(exposure, axis=1), "scen") / (scen * lax.axis_size("scen"))
    return exposure, mean


def solution(mesh):
    in_specs = (
        P(None, "scen", "trade"), P("trade", None), P(), P(None, "trade"),
        P("trade"), P("trade"), P("trade"), P("trade"),
    )
    out_specs = (P(None, "scen", "trade"), P(None, "trade"))
    return jax.shard_map(
        on_device, mesh=mesh, in_specs=in_specs, out_specs=out_specs, check_vma=False
    )
```

time: 813 us -> 364 us (0.45)
  waiting for transfers between devices: 636 us -> 187 us
  matrix products: 86.6 us -> 9 us
  Pallas kernels: 0 us -> 75.6 us
  local copies, waits for them, and re-layouts: 29.6 us -> 40.2 us
  other arithmetic: 12.2 us -> 1.96 us
    psum x1 -> x0, waiting for transfers between devices: 397 us -> none  [on_device(): shock_sums = lax.psum(partials, 'trade')]
    dot_general x18 -> x1, matrix products: 86.6 us -> 9 us  [on_device(): partial = jnp.dot(normal_draws, covariance_root, preferred_element_type=F32)]
    pallas_call x0 -> x1, Pallas kernels: none -> 75.6 us  [values_and_nets(): pl.pallas_call(value_kernel, out_shape=jax.ShapeDtypeStruct((CHUNKS, SETS...]
    reduce_scatter x2 -> x1, waiting for transfers between devices: 239 us -> 187 us  [on_device(): lax.psum_scatter(partial, 'trade', scatter_dimension=0, tiled=False)]
    dynamic_slice x48 -> x0, local copies, waits for them, and re-layouts: 25.6 us -> none  [the longest x16 12.2 us: block_step(): lax.dynamic_slice_in_dim(deal_agreement_group, position_start, tile_field...]
    reshape x0 -> x3, local copies, waits for them, and re-layouts: none -> 22.3 us  [the longest x1 20.4 us: on_device(): partial = partial.reshape(dates, NY, CHUNKS, span, NZ * NX, COLS, LANES)]
    transpose x0 -> x2, local copies, waits for them, and re-layouts: none -> 14.3 us  [the longest x1 14.2 us: on_device(): partial = partial.transpose(4, 1, 2, 5, 0, 3, 6)]
    convert_element_type x1 -> x0, other arithmetic: 9.45 us -> none  [on_device(): level_list = [factor_state.astype(jnp.bfloat16)]]
  transfers between devices with their start and end apart: 3 -> 1, of which waited for: 3 -> 1; matrix products, arithmetic and copies ran while one was open for 7% -> 0% of each run, Pallas kernels for 0% -> 0%
where the time goes in v1:
time: 364 us; the launch traced here: 363 us
  waiting for transfers between devices  187 us (51%)
  Pallas kernels  75.6 us (21%)
  local copies, waits for them, and re-layouts  40.2 us (11%)
  blocking collectives  34 us (9%)
  between operations  14.7 us (4%)
  matrix products  9 us (2%)
    reduce_scatter x1, waiting for transfers between devices, on_device(): lax.psum_scatter(partial, 'trade', scatter_dimension=0, tiled=False)  187 us
    pallas_call x1, Pallas kernels, values_and_nets(): pl.pallas_call(value_kernel, out_shape=jax.ShapeDtypeStruct((CHUNKS, SETS...  75.6 us
    psum x1, blocking collectives, on_device(): lax.psum(jnp.sum(exposure, axis=1), 'scen') / (scen * lax.axis_size('scen'))  34 us
    reshape x1, local copies, waits for them, and re-layouts, on_device(): partial = partial.reshape(dates, NY, CHUNKS, span, NZ * NX, COLS, LANES)  20.4 us
    transpose x1, local copies, waits for them, and re-layouts, on_device(): partial = partial.transpose(4, 1, 2, 5, 0, 3, 6)  14.2 us
    dot_general x1, matrix products, on_device(): partial = jnp.dot(normal_draws, covariance_root, preferred_element_type=F32)  9 us
  transfers between devices with their start and end apart: 1, of which 1 were waited for; matrix products, arithmetic and copies ran while one was open for 0% of the time, Pallas kernels for 0%

profile of v1, /device:TPU:1, one launch (start us, length us, event | category | flops | bytes accessed | tf_op | source)
XLA Modules:
  0.0 362.9 jit_solution(6727688011438585658)
XLA Ops:
  7.2 0.0 copy-start
  7.2 0.0 reduce-scatter.2.cloned.1.call-start
  7.2 1.2 copy-done
  8.4 9.0 %fusion = f32[2,512,4096]{2,1,0:T(8,128)} fusion(bf16[2,512,128]{2,1,0:T(8,128)(2,1)} %param.8, bf16[128,4096]{1,0:T(8,128)(2,1)S(1)} %copy-done), kind=kOutput, calls=%fused_computation | convolution fusion | flops 1073741824 | bytes 18087936 | tf_op jit(solution)/shard_map/dot_general | solution.py:280
  17.4 20.4 %reshape.35 = f32[2,4,4,32,8,4,128]{6,5,4,3,2,1,0:T(4,128)} reshape(f32[2,512,4096]{2,1,0:T(8,128)} %fusion) | data formatting | bytes 33554432 | tf_op jit(solution)/shard_map/reshape | solution.py:281
  37.8 14.2 %copy.12 = f32[8,4,4,4,2,32,128]{6,5,4,3,2,1,0:T(8,128)} copy(f32[8,4,4,4,2,32,128]{6,3,0,5,2,1,4:T(4,128)} %bitcast.21) | data formatting | bytes 33554432 | tf_op jit(solution)/shard_map/transpose | solution.py:282
  52.0 0.0 reduce-scatter.2.cloned.1.call-update
  52.7 0.7 dynamic-slice_bitcast_fusion
  53.4 187.4 %reduce-scatter.2.cloned.1.call-done = f32[1,4,4,2,32,128]{5,4,3,2,1,0:T(8,128)} async-done(((f32[32,4,4,2,32,128]{5,4,3,2,1,0:T(8,128)}), f32[1,4,4,2,32,128]{5,4,3,2,1,0:T(8,128)}) %reduce-scatter.2.cloned.1.call-update) | async-done | bytes 524304 | tf_op jit(solution)/shard_map/reduce_scatter | solution.py:284
  240.8 1.0 slice.15
  241.8 1.1 fusion.2
  242.9 0.7 pad_maximum_fusion
  243.6 0.0 copy-start.1
  243.6 75.6 %value_nets.1 = f32[4,16,256]{2,1,0:T(8,128)} custom-call(bf16[4,4,64,128]{3,2,1,0:T(8,128)(2,1)} %bitcast.25, bf16[4096,2048]{1,0:T(8,128)(2,1)} %sens_hbm.1, f32[1,2048]{1,0:T(1,128)} %bitcast.27, f32[1,2048]{1,0:T(1,128)} %bitcast.28, s32[1,2048]{1,0:T(1,128)} %bitcast.29, s32[1,1]{1,0:T(1,128)} %bitcast.19.live_ref), custom_call_target="tpu_custom_call" | custom-call | flops 19327352832 | bytes 17825792 | tf_op jit(solution)/shard_map/value_nets/pallas_call | solution.py:241
  319.2 1.1 reshape.42
  320.3 0.2 bitcast_reduce_fusion
  320.4 0.2 copy.13
  320.6 0.8 reshape.43
  321.4 34.0 %psum.7 = f32[2,16]{0,1:T(8,128)S(1)} all-reduce(f32[2,16]{0,1:T(8,128)S(1)} %bitcast_reduce_fusion), channel_id=1, replica_groups=mesh['scen'=4,'trade'=32] {'scen'}, use_global_device_ids=true, to_apply=%region_2.3 | all-reduce | flops 32 | bytes 256 | tf_op jit(solution)/shard_map/psum | solution.py:299
  355.4 0.6 copy.14
  356.1 0.0 copy-done.1
  (1 shorter events, 0.0 us)
Async XLA Ops:
  7.2 1.2 copy-start
  7.2 233.6 %reduce-scatter.2.cloned.1.call-start = ((), (), s32[]{:S(2)}) async-start(), calls=%async_computation.1 | async-start | bytes 17301504 | tf_op jit(solution)/shard_map/reduce_scatter | solution.py:284
  243.6 112.5 %copy-start.1 = (bf16[128,4096]{1,0:T(8,128)(2,1)S(1)}, bf16[128,4096]{1,0:T(8,128)(2,1)}, u32[]{:S(2)}) copy-start(bf16[128,4096]{1,0:T(8,128)(2,1)} %param.9) | copy-start | bytes 3145732
Sparse Core Ops, SparseCore 0:
  52.1 188.6 reduce-scatter.1

commit v2 on v1

v2 whole, which is shorter than its diff:
```python
import functools
import jax
import jax.numpy as jnp
from jax import lax
from jax.experimental import pallas as pl
from jax.experimental.pallas import tpu as pltpu
from jax.sharding import PartitionSpec as P

F32, BF16 = jnp.float32, jnp.bfloat16
SETS_DEV = 16
NZ, NX, NY = 2, 4, 4
N_TRADE = NZ * NX * NY
CHUNKS = 4
COLS = 4
ROWS = 64
LANES = 128
TILE = 256
PARTS = (
    ((0, 3), (0, 32), ("z", "y", "x")),
    ((0, 3), (32, 32), ("z", "x", "y")),
    ((3, 1), (0, 64), ("x", "y", "z")),
)
STEPS = 5
DRAW_ORDERS = (("z", "x"), ("x", "z"))
DRAW_STEPS = 3
SLOTS = 10


def trade_place():
    me = lax.axis_index("trade")
    return {"z": me // (NX * NY), "x": (me // NY) % NX, "y": me % NY}


def trade_index(place):
    return (place["z"] * NX + place["x"]) * NY + place["y"]


def moved(place, axis, by):
    size = {"z": NZ, "x": NX, "y": NY}[axis]
    return dict(place, **{axis: (place[axis] + by) % size})


def part_steps(place, order):
    have = dict(place)
    steps = []
    for axis in order:
        if axis == "z":
            steps.append(
                (
                    [(dict(have), None, moved(place, "z", 1))],
                    [(dict(have, z=1 - place["z"]), None)],
                )
            )
        else:
            right, left = moved(place, axis, 1), moved(place, axis, 3)
            far = moved(place, axis, 2)
            at = lambda where: dict(have, **{axis: where[axis]})
            steps.append(
                (
                    [(at(place), None, right), (at(place), None, left)],
                    [(at(left), None), (at(right), None)],
                )
            )
            steps.append(
                (
                    [(at(left), 0, right), (at(right), 1, left)],
                    [(at(far), 0), (at(far), 1)],
                )
            )
        have[axis] = None
    return steps


def softplus(a):
    return jnp.maximum(a, 0.0) + jnp.log1p(jnp.exp(-jnp.abs(a)))


def factor_block(col, owner):
    return 8 * col + (owner if col % 2 == 0 else 7 - owner)


def column_home(col):
    return {3: (0, 0), 0: (0, 8), 2: (1, 0), 1: (1, 6)}[col]


def exposure_kernel(
    draws_hbm, root_hbm, sens_hbm, pull_ref, shift_ref, principal_ref, group_ref, live_ref,
    out_ref, mean_ref,
    draws, root, book, sens, member, weight, net, net_out, net_in, mean_in,
    draw_send, draw_recv, draw_ring_send, draw_ring_recv,
    root_send, root_recv, root_ring_send, root_ring_recv, twin_send, twin_recv,
    send_sems, recv_sems, own_sems, sens_sem, net_send_sem, net_recv_sems,
    mean_send, mean_recv,
):
    place = trade_place()
    me = trade_index(place)
    zx = place["z"] * NX + place["x"]
    scen = lax.axis_index("scen")
    scens = lax.axis_size("scen")
    core = scen % 2
    twin = scen + 1 - 2 * core
    positions = sens.shape[1]
    sets = member.shape[0]
    span = draws_hbm.shape[1] // NY

    def remote(src, dst, send, recv, **target):
        return pltpu.make_async_remote_copy(
            src_ref=src, dst_ref=dst, send_sem=send, recv_sem=recv,
            device_id=target, device_id_type=pl.DeviceIdType.MESH,
        )

    barrier = pltpu.get_barrier_semaphore()

    @pl.loop(1, N_TRADE)
    def _(step):
        pl.semaphore_signal(
            barrier, inc=1, device_id={"trade": (me + step) % N_TRADE},
            device_id_type=pl.DeviceIdType.MESH,
        )

    @pl.loop(1, scens)
    def _(step):
        pl.semaphore_signal(
            barrier, inc=1, device_id={"scen": (scen + step) % scens},
            device_id_type=pl.DeviceIdType.MESH,
        )

    pl.semaphore_wait(barrier, N_TRADE - 1 + scens - 1)

    def draw_rows(y):
        return draws_hbm.at[:, pl.ds(y * span, span), :]

    def draw_copy(by, source):
        return remote(
            draw_rows((place["y"] + by) % NY), draws.at[place["z"], place["x"], source],
            draw_send.at[by - 1], draw_recv.at[by - 1],
            trade=trade_index(moved(place, "y", by)),
        )

    own_draws = pltpu.make_async_copy(
        draw_rows(place["y"]), draws.at[place["z"], place["x"], place["y"]], own_sems.at[0]
    )
    own_draws.start()
    for by in range(1, NY):
        draw_copy(by, place["y"]).start()

    high_count, low_count = 8 - 2 * core, 2 + 2 * core
    kinds = ((3 - core, high_count, 0), (core, low_count, high_count))

    def root_block(kind, owner):
        col = kinds[kind][0]
        block = 8 * col + jnp.where(col % 2 == 0, owner, 7 - owner)
        return root_hbm.at[:, pl.ds(pl.multiple_of(block * LANES, LANES), LANES)]

    def root_slot(kind, source):
        return root.at[core, kinds[kind][2] + source, place["y"]]

    def root_copy(kind, owner, source):
        return remote(
            root_block(kind, owner), root_slot(kind, source),
            root_send.at[kind, owner], root_recv.at[kind, source],
            trade=owner * NY + place["y"],
        )

    def own_root(kind):
        return pltpu.make_async_copy(root_block(kind, zx), root_slot(kind, zx), own_sems.at[1 + kind])

    for kind in range(2):
        @pl.when(zx < kinds[kind][1])
        def _(kind=kind):
            own_root(kind).start()

            @pl.loop(1, NZ * NX)
            def _(step):
                root_copy(kind, (zx + step) % (NZ * NX), zx).start()

    fetch = pltpu.make_async_copy(sens_hbm, sens, sens_sem)
    fetch.start()

    draw_plans = [part_steps(place, order) for order in DRAW_ORDERS]

    def draw_ring(step, kind):
        for date, plan in enumerate(draw_plans):
            sends, recvs = plan[step]
            for way in range(len(sends)):
                coords, half = (sends if kind == "send" else recvs)[way][:2]
                target = sends[way][2]
                row, rows = 0, span
                if half is not None:
                    rows = span // 2
                    row = half * rows
                pick = [slice(None) if coords[a] is None else coords[a] for a in "zx"]
                ref = draws.at[pick[0], pick[1], :, date, pl.ds(row, rows), :]
                yield remote(
                    ref, ref, draw_ring_send.at[date, step, way], draw_ring_recv.at[date, step, way],
                    trade=trade_index(target),
                )

    def root_ring(step, kind):
        y = place["y"]
        right, left = moved(place, "y", 1), moved(place, "y", 3)
        far = (y + 2) % NY
        half = SLOTS // 2
        if step == 0:
            at = {"send": (y, y), "recv": (left["y"], right["y"])}[kind]
            refs = [root.at[core, :, a] for a in at]
        else:
            at = {"send": (left["y"], right["y"]), "recv": (far, far)}[kind]
            refs = [root.at[core, pl.ds(half * way, half), a] for way, a in enumerate(at)]
        for way, target in enumerate((right, left)):
            yield remote(
                refs[way], refs[way], root_ring_send.at[step, way], root_ring_recv.at[step, way],
                trade=trade_index(target),
            )

    def twin_copy(by, from_core):
        ref = root.at[from_core, :, (place["y"] + by) % NY]
        return remote(ref, ref, twin_send.at[by], twin_recv.at[by], scen=twin)

    weight[...] = jnp.where(
        lax.broadcasted_iota(jnp.int32, (1, positions), 1) < live_ref[...],
        principal_ref[...], 0.0,
    )

    own_draws.wait()
    for by in range(1, NY):
        draw_copy(by, (place["y"] + NY - by) % NY).wait_recv()
    for copy in draw_ring(0, "send"):
        copy.start()

    for kind in range(2):
        @pl.when(zx < kinds[kind][1])
        def _(kind=kind):
            own_root(kind).wait()

        @pl.loop(0, NZ * NX)
        def _(source, kind=kind):
            @pl.when(jnp.logical_and(source < kinds[kind][1], source != zx))
            def _():
                root_copy(kind, zx, source).wait_recv()
    for copy in root_ring(0, "send"):
        copy.start()
    twin_copy(0, core).start()

    for copy in draw_ring(0, "recv"):
        copy.wait_recv()
    for copy in draw_ring(1, "send"):
        copy.start()

    for copy in root_ring(0, "recv"):
        copy.wait_recv()
    for copy in root_ring(1, "send"):
        copy.start()
    twin_copy(1, core).start()
    twin_copy(3, core).start()

    for copy in draw_ring(1, "recv"):
        copy.wait_recv()
    for copy in draw_ring(2, "send"):
        copy.start()

    @pl.loop(0, positions // TILE)
    def _(tile):
        at = pl.ds(pl.multiple_of(tile * TILE, TILE), TILE)
        labels = lax.broadcasted_iota(jnp.int32, (sets, TILE), 0)
        member[:, at] = (labels == group_ref[:, at]).astype(F32).astype(BF16)

    for copy in root_ring(1, "recv"):
        copy.wait_recv()
    twin_copy(2, core).start()
    for by in range(NY):
        twin_copy(by, 1 - core).wait_recv()
    for copy in draw_ring(2, "recv"):
        copy.wait_recv()

    dates = draws.shape[3]
    part_rows = span // CHUNKS
    for col in range(COLS):
        home, slot = column_home(col)
        sources = [(s, y) for s in range(2 * (col + 1)) for y in range(NY)]
        left = jnp.concatenate(
            [draws[s // NX, s % NX, y].reshape(dates * span, LANES) for s, y in sources], axis=1
        )
        right = jnp.concatenate([root[home, slot + s, y] for s, y in sources], axis=0)
        shocks = jnp.dot(left, right, preferred_element_type=F32)
        pull = pull_ref[pl.ds(factor_block(col, zx), 1), :]
        state = jnp.zeros((span, LANES), F32)
        for date in range(dates):
            state = pull * state + shocks[date * span:(date + 1) * span]
            levels = state.astype(BF16)
            for chunk in range(CHUNKS):
                book[
                    chunk, place["z"], place["x"], col, place["y"],
                    pl.ds(date * part_rows, part_rows), :,
                ] = levels[chunk * part_rows:(chunk + 1) * part_rows]

    plans = [part_steps(place, order) for _, _, order in PARTS]

    def view(part, chunk, coords, half):
        (col, cols), (row, rows), _ = PARTS[part]
        if half is not None:
            rows = rows // 2
            row = row + half * rows
        pick = [slice(None) if coords[a] is None else coords[a] for a in "zxy"]
        return book.at[chunk, pick[0], pick[1], pl.ds(col, cols), pick[2], pl.ds(row, rows), :]

    def descriptors(part, step, chunk, kind):
        sends, recvs = plans[part][step]
        for way in range(len(sends)):
            if kind == "send":
                coords, half, target = sends[way]
            else:
                coords, half = recvs[way]
                target = place
            ref = view(part, chunk, coords, half)
            yield remote(
                ref, ref, send_sems.at[chunk, part, step, way], recv_sems.at[chunk, part, step, way],
                trade=trade_index(target),
            )

    def start(step, chunk):
        for part in range(len(PARTS)):
            for copy in descriptors(part, step, chunk, "send"):
                copy.start()

    def arrived(step, chunk):
        for part in range(len(PARTS)):
            for copy in descriptors(part, step, chunk, "recv"):
                copy.wait_recv()

    @pl.loop(0, CHUNKS)
    def _(chunk):
        start(0, chunk)

    for step in (1, 2):
        @pl.loop(0, CHUNKS)
        def _(chunk, step=step):
            arrived(step - 1, chunk)
            start(step, chunk)

    fetch.wait()

    def net_copy(chunk, target):
        return remote(
            net_out.at[chunk, target], net_in.at[chunk, me],
            net_send_sem, net_recv_sems.at[chunk], trade=target,
        )

    def compute(chunk):
        net[...] = jnp.zeros_like(net)
        levels = jnp.concatenate(
            [
                book[chunk, owner // NX, owner % NX, col].reshape(NY * ROWS, LANES)
                for col in range(COLS) for owner in range(NZ * NX)[:: 1 - 2 * (col % 2)]
            ],
            axis=1,
        )

        @pl.loop(0, positions // TILE)
        def _(tile):
            at = pl.ds(pl.multiple_of(tile * TILE, TILE), TILE)
            moneyness = jnp.dot(levels, sens[:, at], preferred_element_type=F32)
            values = weight[:, at] * softplus(moneyness + shift_ref[:, at])
            net[...] += lax.dot_general(
                member[:, at], values.astype(BF16), (((1,), (1,)), ((), ())),
                preferred_element_type=F32,
            )

        net_out[chunk] = net[...].astype(BF16).reshape(N_TRADE, SETS_DEV, NY * ROWS)

        @pl.loop(1, N_TRADE)
        def _(step):
            net_copy(chunk, (me + step) % N_TRADE).start()

        net_in[chunk, me] = net_out[chunk, me]

    @pl.loop(0, CHUNKS + 2)
    def _(tick):
        @pl.when(tick < CHUNKS)
        def _():
            arrived(2, tick)
            start(3, tick)

        @pl.when(jnp.logical_and(tick >= 1, tick < CHUNKS + 1))
        def _():
            arrived(3, tick - 1)
            start(4, tick - 1)

        @pl.when(tick >= 2)
        def _():
            arrived(4, tick - 2)
            compute(tick - 2)

    @pl.loop(0, CHUNKS)
    def _(chunk):
        for part in range(len(PARTS)):
            for step in range(STEPS):
                for copy in descriptors(part, step, chunk, "send"):
                    copy.wait_send()

        whole = remote(
            net_out.at[chunk, pl.ds(0, N_TRADE - 1)], net_in.at[chunk, pl.ds(0, N_TRADE - 1)],
            net_send_sem, net_recv_sems.at[chunk], trade=me,
        )
        whole.wait_send()
        whole.wait_recv()
        total = jnp.zeros((SETS_DEV, NY * ROWS), F32)
        for sender in range(N_TRADE):
            total = total + net_in[chunk, sender].astype(F32)
        net[pl.ds(pl.multiple_of(chunk * SETS_DEV, SETS_DEV), SETS_DEV), :] = jnp.maximum(total, 0.0)

    lane = lax.broadcasted_iota(jnp.int32, (SETS_DEV, LANES), 1)
    sums = jnp.zeros((SETS_DEV, LANES), F32)
    for date in range(dates):
        strip = jnp.concatenate(
            [
                net[chunk * SETS_DEV:(chunk + 1) * SETS_DEV, y * ROWS + date * part_rows:][:, :part_rows]
                for y in range(NY) for chunk in range(CHUNKS)
            ],
            axis=1,
        )
        out_ref[date] = strip
        sums = jnp.where(lane == date, jnp.sum(strip, axis=1, keepdims=True), sums)
    mean_in[scen] = sums

    def mean_copy(by, slot):
        return remote(
            mean_in.at[slot], mean_in.at[slot], mean_send.at[by - 1], mean_recv.at[by - 1],
            scen=(scen + by) % scens,
        )

    for by in range(1, scens):
        mean_copy(by, scen).start()

    for by in range(1, NY):
        draw_copy(by, place["y"]).wait_send()
    for step in range(DRAW_STEPS):
        for copy in draw_ring(step, "send"):
            copy.wait_send()
    for kind in range(2):
        @pl.when(zx < kinds[kind][1])
        def _(kind=kind):
            @pl.loop(1, NZ * NX)
            def _(step):
                root_copy(kind, (zx + step) % (NZ * NX), zx).wait_send()
    for step in range(2):
        for copy in root_ring(step, "send"):
            copy.wait_send()
    for by in range(NY):
        twin_copy(by, core).wait_send()

    for by in range(1, scens):
        mean_copy(by, (scen + scens - by) % scens).wait_recv()
        mean_copy(by, scen).wait_send()
    mean_ref[...] = jnp.sum(mean_in[...], axis=0) / (scens * NY * span)


def exposures(draws, root, sensitivity, pull, shift, principal, group, live):
    dates, scen, _ = draws.shape
    positions = sensitivity.shape[1]
    sets = SETS_DEV * N_TRADE
    span = scen // NY
    vmem = pl.BlockSpec(memory_space=pltpu.VMEM)
    hbm = pl.BlockSpec(memory_space=pl.ANY)
    dma = pltpu.SemaphoreType.DMA
    return pl.pallas_call(
        exposure_kernel,
        out_shape=(
            jax.ShapeDtypeStruct((dates, SETS_DEV, scen), F32),
            jax.ShapeDtypeStruct((SETS_DEV, LANES), F32),
        ),
        in_specs=[hbm, hbm, hbm, vmem, vmem, vmem, vmem, vmem],
        out_specs=(vmem, vmem),
        scratch_shapes=[
            pltpu.VMEM((NZ, NX, NY, dates, span, LANES), BF16),
            pltpu.VMEM((2, SLOTS, NY, LANES, LANES), BF16),
            pltpu.VMEM((CHUNKS, NZ, NX, COLS, NY, ROWS, LANES), BF16),
            pltpu.VMEM(sensitivity.shape, BF16),
            pltpu.VMEM((sets, positions), BF16),
            pltpu.VMEM((1, positions), F32),
            pltpu.VMEM((sets, NY * ROWS), F32),
            pltpu.VMEM((CHUNKS, N_TRADE, SETS_DEV, NY * ROWS), BF16),
            pltpu.VMEM((CHUNKS, N_TRADE, SETS_DEV, NY * ROWS), BF16),
            pltpu.VMEM((lax.axis_size("scen"), SETS_DEV, LANES), F32),
            dma((NY - 1,)), dma((NY - 1,)),
            dma((dates, DRAW_STEPS, 2)), dma((dates, DRAW_STEPS, 2)),
            dma((2, NZ * NX)), dma((2, NZ * NX)),
            dma((2, 2)), dma((2, 2)), dma((NY,)), dma((NY,)),
            dma((CHUNKS, len(PARTS), STEPS, 2)), dma((CHUNKS, len(PARTS), STEPS, 2)),
            dma((3,)), dma, dma, dma((CHUNKS,)),
            dma((lax.axis_size("scen") - 1,)), dma((lax.axis_size("scen") - 1,)),
        ],
        compiler_params=pltpu.CompilerParams(
            collective_id=1, has_side_effects=True, vmem_limit_bytes=58 * 2**20
        ),
        cost_estimate=pl.CostEstimate(
            flops=2 * 1024 * positions * (4096 + sets), bytes_accessed=17 << 20, transcendentals=0
        ),
        name="exposures",
    )(
        draws, root, sensitivity, pull.reshape(-1, LANES), shift.reshape(1, -1),
        principal.reshape(1, -1), group.reshape(1, -1), live.reshape(1, 1),
    )


def on_device(
    normal_draws, covariance_root, mean_pullback, sensitivity_tensor,
    moneyness_shift, signed_principal, deal_agreement_group, active_position_number,
):
    exposure, mean = exposures(
        normal_draws, covariance_root, sensitivity_tensor, mean_pullback, moneyness_shift,
        signed_principal, deal_agreement_group, active_position_number,
    )
    return exposure.transpose(0, 2, 1), mean[:, : normal_draws.shape[0]].T


def solution(mesh):
    in_specs = (
        P(None, "scen", "trade"), P("trade", None), P(), P(None, "trade"),
        P("trade"), P("trade"), P("trade"), P("trade"),
    )
    out_specs = (P(None, "scen", "trade"), P(None, "trade"))
    return jax.shard_map(
        on_device, mesh=mesh, in_specs=in_specs, out_specs=out_specs, check_vma=False
    )
```

time: 364 us -> 130 us (0.36)
  waiting for transfers between devices: 187 us -> 0 us
  Pallas kernels: 75.6 us -> 126 us
  local copies, waits for them, and re-layouts: 40.2 us -> 2.81 us
  blocking collectives: 34 us -> 0 us
  between operations: 14.7 us -> 1.29 us
  matrix products: 9 us -> 0 us
    reduce_scatter x1 -> x0, waiting for transfers between devices: 187 us -> none  [on_device(): lax.psum_scatter(partial, 'trade', scatter_dimension=0, tiled=False)]
    pallas_call x1, Pallas kernels: 75.6 us -> 126 us  [exposures(): pl.pallas_call(exposure_kernel, out_shape=(jax.ShapeDtypeStruct((dates, S...]
    psum x1 -> x0, blocking collectives: 34 us -> none  [on_device(): lax.psum(jnp.sum(exposure, axis=1), 'scen') / (scen * lax.axis_size('scen'))]
    reshape x3 -> x0, local copies, waits for them, and re-layouts: 22.3 us -> none  [the longest x1 20.4 us: on_device(): partial = partial.reshape(dates, NY, CHUNKS, span, NZ * NX, COLS, LANES)]
    transpose x2 -> x1, local copies, waits for them, and re-layouts: 14.3 us -> 0.7 us  [on_device(): return (exposure.transpose(0, 2, 1), mean[:, :normal_draws.shape[0]].T)]
    dot_general x1 -> x0, matrix products: 9 us -> none  [on_device(): partial = jnp.dot(normal_draws, covariance_root, preferred_element_type=F32)]
  transfers between devices with their start and end apart: 1 -> 0, of which waited for: 1 -> 0; matrix products, arithmetic and copies ran while one was open for 0% -> 0% of each run, Pallas kernels for 0% -> 0%
where the time goes in v2:
time: 130 us
  Pallas kernels  126 us (97%)
  local copies, waits for them, and re-layouts  2.81 us (2%)
    pallas_call x1, Pallas kernels, exposures(): pl.pallas_call(exposure_kernel, out_shape=(jax.ShapeDtypeStruct((dates, S...  126 us

profile of v2, /device:TPU:1, one launch (start us, length us, event | category | flops | bytes accessed | tf_op | source)
XLA Modules:
  0.0 130.2 jit_solution(13713320564223170682)
XLA Ops:
  1.3 126.1 %exposures.1 = (f32[2,16,512]{2,1,0:T(8,128)}, f32[16,128]{1,0:T(8,128)}) custom-call(bf16[2,512,128]{2,1,0:T(8,128)(2,1)} %draws_hbm.1, bf16[128,4096]{1,0:T(8,128)(2,1)} %root_hbm.1, bf16[4096,2048]{1,0:T(8,128)(2,1)} %sens_hbm.1, f32[32,128]{1,0:T(8,128)} %bitcast.10, f32[1,2048]{1,0:T(1,128)} %bitcast.11, f32[1,2048]{1,0:T(1,128)} %bitcast.12, ...), custom_call_target="tpu_custom_call" | custom-call | flops 19327352832 | bytes 17825792 | tf_op jit(solution)/shard_map/exposures/pallas_call | solution.py:466
  127.4 0.7 slice_bitcast_fusion
  128.1 0.6 copy.10
  128.8 1.5 %copy.13 = f32[2,512,16]{1,2,0:T(8,128)} copy(f32[2,512,16]{1,2,0:T(8,128)} %bitcast.9) | data formatting | bytes 131072

commit v3 on v2

--- a/solution.py
+++ b/solution.py
@@ -14,7 +14,8 @@
 COLS = 4
 ROWS = 64
 LANES = 128
-TILE = 256
+TILE = 512
+HALVES = 2
 PARTS = (
     ((0, 3), (0, 32), ("z", "y", "x")),
     ((0, 3), (32, 32), ("z", "x", "y")),
@@ -72,7 +73,7 @@
 
 
 def softplus(a):
-    return jnp.maximum(a, 0.0) + jnp.log1p(jnp.exp(-jnp.abs(a)))
+    return jnp.maximum(a, 0.0) + jnp.log(1.0 + jnp.exp(-jnp.abs(a)))
 
 
 def factor_block(col, owner):
@@ -86,7 +87,7 @@
 def exposure_kernel(
     draws_hbm, root_hbm, sens_hbm, pull_ref, shift_ref, principal_ref, group_ref, live_ref,
     out_ref, mean_ref,
-    draws, root, book, sens, member, weight, net, net_out, net_in, mean_in,
+    draws, root, book, sens, member, weight, net, prices, net_out, net_in, mean_in,
     draw_send, draw_recv, draw_ring_send, draw_ring_recv,
     root_send, root_recv, root_ring_send, root_ring_recv, twin_send, twin_recv,
     send_sems, recv_sems, own_sems, sens_sem, net_send_sem, net_recv_sems,
@@ -179,20 +180,22 @@
 
     draw_plans = [part_steps(place, order) for order in DRAW_ORDERS]
 
-    def draw_ring(step, kind):
+    def draw_ring(step, kind, part):
         for date, plan in enumerate(draw_plans):
             sends, recvs = plan[step]
             for way in range(len(sends)):
                 coords, half = (sends if kind == "send" else recvs)[way][:2]
                 target = sends[way][2]
-                row, rows = 0, span
+                rows = span // HALVES
+                row = part * rows
                 if half is not None:
-                    rows = span // 2
-                    row = half * rows
+                    rows = rows // 2
+                    row = row + half * rows
                 pick = [slice(None) if coords[a] is None else coords[a] for a in "zx"]
                 ref = draws.at[pick[0], pick[1], :, date, pl.ds(row, rows), :]
                 yield remote(
-                    ref, ref, draw_ring_send.at[date, step, way], draw_ring_recv.at[date, step, way],
+                    ref, ref, draw_ring_send.at[part, date, step, way],
+                    draw_ring_recv.at[part, date, step, way],
                     trade=trade_index(target),
                 )
 
@@ -225,8 +228,16 @@
     own_draws.wait()
     for by in range(1, NY):
         draw_copy(by, (place["y"] + NY - by) % NY).wait_recv()
-    for copy in draw_ring(0, "send"):
-        copy.start()
+    def draw_start(step, part):
+        for copy in draw_ring(step, "send", part):
+            copy.start()
+
+    def draw_arrived(step, part):
+        for copy in draw_ring(step, "recv", part):
+            copy.wait_recv()
+
+    for part in range(HALVES):
+        draw_start(0, part)
 
     for kind in range(2):
         @pl.when(zx < kinds[kind][1])
@@ -242,10 +253,9 @@
         copy.start()
     twin_copy(0, core).start()
 
-    for copy in draw_ring(0, "recv"):
-        copy.wait_recv()
-    for copy in draw_ring(1, "send"):
-        copy.start()
+    for part in range(HALVES):
+        draw_arrived(0, part)
+        draw_start(1, part)
 
     for copy in root_ring(0, "recv"):
         copy.wait_recv()
@@ -254,10 +264,13 @@
     twin_copy(1, core).start()
     twin_copy(3, core).start()
 
-    for copy in draw_ring(1, "recv"):
+    for part in range(HALVES):
+        draw_arrived(1, part)
+        draw_start(2, part)
+
+    for copy in root_ring(1, "recv"):
         copy.wait_recv()
-    for copy in draw_ring(2, "send"):
-        copy.start()
+    twin_copy(2, core).start()
 
     @pl.loop(0, positions // TILE)
     def _(tile):
@@ -265,34 +278,36 @@
         labels = lax.broadcasted_iota(jnp.int32, (sets, TILE), 0)
         member[:, at] = (labels == group_ref[:, at]).astype(F32).astype(BF16)
 
-    for copy in root_ring(1, "recv"):
-        copy.wait_recv()
-    twin_copy(2, core).start()
     for by in range(NY):
         twin_copy(by, 1 - core).wait_recv()
-    for copy in draw_ring(2, "recv"):
-        copy.wait_recv()
 
     dates = draws.shape[3]
     part_rows = span // CHUNKS
-    for col in range(COLS):
-        home, slot = column_home(col)
-        sources = [(s, y) for s in range(2 * (col + 1)) for y in range(NY)]
-        left = jnp.concatenate(
-            [draws[s // NX, s % NX, y].reshape(dates * span, LANES) for s, y in sources], axis=1
-        )
-        right = jnp.concatenate([root[home, slot + s, y] for s, y in sources], axis=0)
-        shocks = jnp.dot(left, right, preferred_element_type=F32)
-        pull = pull_ref[pl.ds(factor_block(col, zx), 1), :]
-        state = jnp.zeros((span, LANES), F32)
-        for date in range(dates):
-            state = pull * state + shocks[date * span:(date + 1) * span]
-            levels = state.astype(BF16)
-            for chunk in range(CHUNKS):
-                book[
-                    chunk, place["z"], place["x"], col, place["y"],
-                    pl.ds(date * part_rows, part_rows), :,
-                ] = levels[chunk * part_rows:(chunk + 1) * part_rows]
+
+    def make_levels(part):
+        rows = span // HALVES
+        for col in range(COLS):
+            home, slot = column_home(col)
+            sources = [(s, y) for s in range(2 * (col + 1)) for y in range(NY)]
+            left = jnp.concatenate(
+                [
+                    draws[s // NX, s % NX, y, :, pl.ds(part * rows, rows), :].reshape(dates * rows, LANES)
+                    for s, y in sources
+                ],
+                axis=1,
+            )
+            right = jnp.concatenate([root[home, slot + s, y] for s, y in sources], axis=0)
+            shocks = jnp.dot(left, right, preferred_element_type=F32)
+            pull = pull_ref[pl.ds(factor_block(col, zx), 1), :]
+            state = jnp.zeros((rows, LANES), F32)
+            for date in range(dates):
+                state = pull * state + shocks[date * rows:(date + 1) * rows]
+                levels = state.astype(BF16)
+                for chunk in range(CHUNKS // HALVES):
+                    book[
+                        part * (CHUNKS // HALVES) + chunk, place["z"], place["x"], col, place["y"],
+                        pl.ds(date * part_rows, part_rows), :,
+                    ] = levels[chunk * part_rows:(chunk + 1) * part_rows]
 
     plans = [part_steps(place, order) for _, _, order in PARTS]
 
@@ -328,17 +343,12 @@
             for copy in descriptors(part, step, chunk, "recv"):
                 copy.wait_recv()
 
-    @pl.loop(0, CHUNKS)
-    def _(chunk):
-        start(0, chunk)
-
-    for step in (1, 2):
-        @pl.loop(0, CHUNKS)
-        def _(chunk, step=step):
-            arrived(step - 1, chunk)
-            start(step, chunk)
-
-    fetch.wait()
+    for part in range(HALVES):
+        draw_arrived(2, part)
+        make_levels(part)
+        for chunk in range(CHUNKS // HALVES):
+            start(0, part * (CHUNKS // HALVES) + chunk)
+
 
     def net_copy(chunk, target):
         return remote(
@@ -356,16 +366,34 @@
             axis=1,
         )
 
-        @pl.loop(0, positions // TILE)
-        def _(tile):
-            at = pl.ds(pl.multiple_of(tile * TILE, TILE), TILE)
-            moneyness = jnp.dot(levels, sens[:, at], preferred_element_type=F32)
-            values = weight[:, at] * softplus(moneyness + shift_ref[:, at])
+        def strip(tile):
+            return pl.ds(pl.multiple_of(tile * TILE, TILE), TILE)
+
+        def price(tile, slot):
+            prices[slot] = jnp.dot(levels, sens[:, strip(tile)], preferred_element_type=F32)
+
+        def settle(tile, slot):
+            at = strip(tile)
+            values = weight[:, at] * softplus(prices[slot] + shift_ref[:, at])
             net[...] += lax.dot_general(
                 member[:, at], values.astype(BF16), (((1,), (1,)), ((), ())),
                 preferred_element_type=F32,
             )
 
+        tiles = positions // TILE
+        price(0, 0)
+
+        @pl.loop(0, tiles // 2 - 1)
+        def _(pair):
+            price(2 * pair + 1, 1)
+            settle(2 * pair, 0)
+            price(2 * pair + 2, 0)
+            settle(2 * pair + 1, 1)
+
+        price(tiles - 1, 1)
+        settle(tiles - 2, 0)
+        settle(tiles - 1, 1)
+
         net_out[chunk] = net[...].astype(BF16).reshape(N_TRADE, SETS_DEV, NY * ROWS)
 
         @pl.loop(1, N_TRADE)
@@ -374,69 +402,33 @@
 
         net_in[chunk, me] = net_out[chunk, me]
 
-    @pl.loop(0, CHUNKS + 2)
+    @pl.loop(0, CHUNKS + STEPS - 1)
     def _(tick):
-        @pl.when(tick < CHUNKS)
+        for step in reversed(range(1, STEPS)):
+            chunk = tick - (step - 1)
+
+            @pl.when(jnp.logical_and(chunk >= 0, chunk < CHUNKS))
+            def _(step=step, chunk=chunk):
+                arrived(step - 1, chunk)
+                start(step, chunk)
+
+        last = tick - (STEPS - 1)
+
+        @pl.when(last == 0)
         def _():
-            arrived(2, tick)
-            start(3, tick)
-
-        @pl.when(jnp.logical_and(tick >= 1, tick < CHUNKS + 1))
+            fetch.wait()
+
+        @pl.when(last >= 0)
         def _():
-            arrived(3, tick - 1)
-            start(4, tick - 1)
-
-        @pl.when(tick >= 2)
-        def _():
-            arrived(4, tick - 2)
-            compute(tick - 2)
-
-    @pl.loop(0, CHUNKS)
-    def _(chunk):
-        for part in range(len(PARTS)):
-            for step in range(STEPS):
-                for copy in descriptors(part, step, chunk, "send"):
-                    copy.wait_send()
-
-        whole = remote(
-            net_out.at[chunk, pl.ds(0, N_TRADE - 1)], net_in.at[chunk, pl.ds(0, N_TRADE - 1)],
-            net_send_sem, net_recv_sems.at[chunk], trade=me,
-        )
-        whole.wait_send()
-        whole.wait_recv()
-        total = jnp.zeros((SETS_DEV, NY * ROWS), F32)
-        for sender in range(N_TRADE):
-            total = total + net_in[chunk, sender].astype(F32)
-        net[pl.ds(pl.multiple_of(chunk * SETS_DEV, SETS_DEV), SETS_DEV), :] = jnp.maximum(total, 0.0)
-
-    lane = lax.broadcasted_iota(jnp.int32, (SETS_DEV, LANES), 1)
-    sums = jnp.zeros((SETS_DEV, LANES), F32)
-    for date in range(dates):
-        strip = jnp.concatenate(
-            [
-                net[chunk * SETS_DEV:(chunk + 1) * SETS_DEV, y * ROWS + date * part_rows:][:, :part_rows]
-                for y in range(NY) for chunk in range(CHUNKS)
-            ],
-            axis=1,
-        )
-        out_ref[date] = strip
-        sums = jnp.where(lane == date, jnp.sum(strip, axis=1, keepdims=True), sums)
-    mean_in[scen] = sums
-
-    def mean_copy(by, slot):
-        return remote(
-            mean_in.at[slot], mean_in.at[slot], mean_send.at[by - 1], mean_recv.at[by - 1],
-            scen=(scen + by) % scens,
-        )
-
-    for by in range(1, scens):
-        mean_copy(by, scen).start()
+            arrived(STEPS - 1, last)
+            compute(last)
 
     for by in range(1, NY):
         draw_copy(by, place["y"]).wait_send()
-    for step in range(DRAW_STEPS):
-        for copy in draw_ring(step, "send"):
-            copy.wait_send()
+    for part in range(HALVES):
+        for step in range(DRAW_STEPS):
+            for copy in draw_ring(step, "send", part):
+                copy.wait_send()
     for kind in range(2):
         @pl.when(zx < kinds[kind][1])
         def _(kind=kind):
@@ -449,10 +441,55 @@
     for by in range(NY):
         twin_copy(by, core).wait_send()
 
+    @pl.loop(0, CHUNKS)
+    def _(chunk):
+        for part in range(len(PARTS)):
+            for step in range(STEPS):
+                for copy in descriptors(part, step, chunk, "send"):
+                    copy.wait_send()
+
+    @pl.loop(0, CHUNKS)
+    def _(chunk):
+        whole = remote(
+            net_out.at[chunk, pl.ds(0, N_TRADE - 1)], net_in.at[chunk, pl.ds(0, N_TRADE - 1)],
+            net_send_sem, net_recv_sems.at[chunk], trade=me,
+        )
+        whole.wait_send()
+        whole.wait_recv()
+        total = jnp.zeros((SETS_DEV, NY * ROWS), F32)
+        for sender in range(N_TRADE):
+            total = total + net_in[chunk, sender].astype(F32)
+        net[pl.ds(pl.multiple_of(chunk * SETS_DEV, SETS_DEV), SETS_DEV), :] = jnp.maximum(total, 0.0)
+
+    mean_in[scen] = jnp.zeros(mean_in.shape[1:], F32)
+    down = lax.broadcasted_iota(jnp.int32, (SETS_DEV, LANES), 0)
+    across = lax.broadcasted_iota(jnp.int32, (SETS_DEV, LANES), 1)
+    for date in range(dates):
+        strip = jnp.concatenate(
+            [
+                net[chunk * SETS_DEV:(chunk + 1) * SETS_DEV, y * ROWS + date * part_rows:][:, :part_rows]
+                for y in range(NY) for chunk in range(CHUNKS)
+            ],
+            axis=1,
+        )
+        out_ref[date] = strip
+        sums = jnp.where(down == across, jnp.sum(strip, axis=1, keepdims=True), 0.0)
+        mean_in[scen, pl.ds(date, 1), :] = jnp.sum(sums, axis=0, keepdims=True)
+
+    def mean_copy(by, slot):
+        return remote(
+            mean_in.at[slot], mean_in.at[slot], mean_send.at[by - 1], mean_recv.at[by - 1],
+            scen=(scen + by) % scens,
+        )
+
+    for by in range(1, scens):
+        mean_copy(by, scen).start()
+
     for by in range(1, scens):
         mean_copy(by, (scen + scens - by) % scens).wait_recv()
         mean_copy(by, scen).wait_send()
-    mean_ref[...] = jnp.sum(mean_in[...], axis=0) / (scens * NY * span)
+    total = jnp.sum(mean_in[...], axis=0) / (scens * NY * span)
+    mean_ref[...] = total[:dates, :SETS_DEV]
 
 
 def exposures(draws, root, sensitivity, pull, shift, principal, group, live):
@@ -467,7 +504,7 @@
         exposure_kernel,
         out_shape=(
             jax.ShapeDtypeStruct((dates, SETS_DEV, scen), F32),
-            jax.ShapeDtypeStruct((SETS_DEV, LANES), F32),
+            jax.ShapeDtypeStruct((dates, SETS_DEV), F32),
         ),
         in_specs=[hbm, hbm, hbm, vmem, vmem, vmem, vmem, vmem],
         out_specs=(vmem, vmem),
@@ -479,11 +516,12 @@
             pltpu.VMEM((sets, positions), BF16),
             pltpu.VMEM((1, positions), F32),
             pltpu.VMEM((sets, NY * ROWS), F32),
+            pltpu.VMEM((2, NY * ROWS, TILE), F32),
             pltpu.VMEM((CHUNKS, N_TRADE, SETS_DEV, NY * ROWS), BF16),
             pltpu.VMEM((CHUNKS, N_TRADE, SETS_DEV, NY * ROWS), BF16),
-            pltpu.VMEM((lax.axis_size("scen"), SETS_DEV, LANES), F32),
+            pltpu.VMEM((lax.axis_size("scen"), 8, LANES), F32),
             dma((NY - 1,)), dma((NY - 1,)),
-            dma((dates, DRAW_STEPS, 2)), dma((dates, DRAW_STEPS, 2)),
+            dma((HALVES, dates, DRAW_STEPS, 2)), dma((HALVES, dates, DRAW_STEPS, 2)),
             dma((2, NZ * NX)), dma((2, NZ * NX)),
             dma((2, 2)), dma((2, 2)), dma((NY,)), dma((NY,)),
             dma((CHUNKS, len(PARTS), STEPS, 2)), dma((CHUNKS, len(PARTS), STEPS, 2)),
@@ -511,7 +549,7 @@
         normal_draws, covariance_root, sensitivity_tensor, mean_pullback, moneyness_shift,
         signed_principal, deal_agreement_group, active_position_number,
     )
-    return exposure.transpose(0, 2, 1), mean[:, : normal_draws.shape[0]].T
+    return exposure.transpose(0, 2, 1), mean
 
 
 def solution(mesh):

time: 130 us -> 119 us (0.915)
  Pallas kernels: 126 us -> 115 us
    pallas_call x1, Pallas kernels: 126 us -> 115 us  [exposures(): pl.pallas_call(exposure_kernel, out_shape=(jax.ShapeDtypeStruct((dates, S...]
where the time goes in v3:
time: 119 us
  Pallas kernels  115 us (97%)
  local copies, waits for them, and re-layouts  2.67 us (2%)
  between operations  1.29 us (1%)
    pallas_call x1, Pallas kernels, exposures(): pl.pallas_call(exposure_kernel, out_shape=(jax.ShapeDtypeStruct((dates, S...  115 us
    unnamed x2, local copies, waits for them, and re-layouts  2.67 us

profile of v3, /device:TPU:1, one launch (start us, length us, event | category | flops | bytes accessed | tf_op | source)
XLA Modules:
  0.0 118.8 jit_solution(14261509592112812737)
XLA Ops:
  1.3 114.9 %exposures.1 = (f32[2,16,512]{2,1,0:T(8,128)}, f32[2,16]{1,0:T(2,128)}) custom-call(bf16[2,512,128]{2,1,0:T(8,128)(2,1)} %draws_hbm.1, bf16[128,4096]{1,0:T(8,128)(2,1)} %root_hbm.1, bf16[4096,2048]{1,0:T(8,128)(2,1)} %sens_hbm.1, f32[32,128]{1,0:T(8,128)} %bitcast.8, f32[1,2048]{1,0:T(1,128)} %bitcast.9, f32[1,2048]{1,0:T(1,128)} %bitcast.10, ...), custom_call_target="tpu_custom_call" | custom-call | flops 19327352832 | bytes 17825792 | tf_op jit(solution)/shard_map/exposures/pallas_call | solution.py:503
  116.2 1.5 %copy.13 = f32[2,512,16]{1,2,0:T(8,128)} copy(f32[2,512,16]{1,2,0:T(8,128)} %bitcast.7) | data formatting | bytes 131072
  117.6 1.2 %copy.14 = f32[2,16]{1,0:T(2,128)} copy(f32[2,16]{1,0:T(2,128)} %get-tuple-element.9) | data formatting | bytes 256

commit v4 on v3

--- a/solution.py
+++ b/solution.py
@@ -72,6 +72,19 @@
     return steps
 
 
+def hand_on(arrivals, sends, pairwise):
+    arrivals, sends = list(arrivals), list(sends)
+    if pairwise:
+        for arrival, send in zip(arrivals, sends):
+            arrival.wait_recv()
+            send.start()
+    else:
+        for arrival in arrivals:
+            arrival.wait_recv()
+        for send in sends:
+            send.start()
+
+
 def softplus(a):
     return jnp.maximum(a, 0.0) + jnp.log(1.0 + jnp.exp(-jnp.abs(a)))
 
@@ -180,8 +193,10 @@
 
     draw_plans = [part_steps(place, order) for order in DRAW_ORDERS]
 
-    def draw_ring(step, kind, part):
-        for date, plan in enumerate(draw_plans):
+    def draw_ring(step, kind, part, only=None):
+        for date, plan in reversed(list(enumerate(draw_plans))):
+            if only is not None and date != only:
+                continue
             sends, recvs = plan[step]
             for way in range(len(sends)):
                 coords, half = (sends if kind == "send" else recvs)[way][:2]
@@ -232,6 +247,13 @@
         for copy in draw_ring(step, "send", part):
             copy.start()
 
+    def draw_advance(step, part):
+        for date, plan in reversed(list(enumerate(draw_plans))):
+            hand_on(
+                draw_ring(step - 1, "recv", part, date), draw_ring(step, "send", part, date),
+                plan[step][0][0][1] is not None,
+            )
+
     def draw_arrived(step, part):
         for copy in draw_ring(step, "recv", part):
             copy.wait_recv()
@@ -254,8 +276,7 @@
     twin_copy(0, core).start()
 
     for part in range(HALVES):
-        draw_arrived(0, part)
-        draw_start(1, part)
+        draw_advance(1, part)
 
     for copy in root_ring(0, "recv"):
         copy.wait_recv()
@@ -265,8 +286,7 @@
     twin_copy(3, core).start()
 
     for part in range(HALVES):
-        draw_arrived(1, part)
-        draw_start(2, part)
+        draw_advance(2, part)
 
     for copy in root_ring(1, "recv"):
         copy.wait_recv()
@@ -333,22 +353,48 @@
                 trade=trade_index(target),
             )
 
-    def start(step, chunk):
+    def start(chunk):
         for part in range(len(PARTS)):
-            for copy in descriptors(part, step, chunk, "send"):
+            for copy in descriptors(part, 0, chunk, "send"):
                 copy.start()
 
-    def arrived(step, chunk):
+    def advance(step, chunk):
         for part in range(len(PARTS)):
-            for copy in descriptors(part, step, chunk, "recv"):
+            hand_on(
+                descriptors(part, step - 1, chunk, "recv"), descriptors(part, step, chunk, "send"),
+                plans[part][step][0][0][1] is not None,
+            )
+
+    def complete(chunk):
+        for part in range(len(PARTS)):
+            for copy in descriptors(part, STEPS - 1, chunk, "recv"):
                 copy.wait_recv()
 
-    for part in range(HALVES):
-        draw_arrived(2, part)
-        make_levels(part)
-        for chunk in range(CHUNKS // HALVES):
-            start(0, part * (CHUNKS // HALVES) + chunk)
-
+    half_chunks = CHUNKS // HALVES
+
+    def both(part, act):
+        @pl.loop(part * half_chunks, (part + 1) * half_chunks)
+        def _(chunk):
+            act(chunk)
+
+    draw_arrived(2, 0)
+    make_levels(0)
+    both(0, start)
+    both(0, functools.partial(advance, 1))
+    draw_arrived(2, 1)
+    make_levels(1)
+    both(1, start)
+    both(0, functools.partial(advance, 2))
+    both(1, functools.partial(advance, 1))
+    advance(3, 0)
+    advance(2, 2)
+    advance(3, 1)
+    advance(2, 3)
+
+    @pl.loop(0, CHUNKS - 2)
+    def _(chunk):
+        advance(4, chunk)
+        advance(3, chunk + 2)
 
     def net_copy(chunk, target):
         return remote(
@@ -402,26 +448,17 @@
 
         net_in[chunk, me] = net_out[chunk, me]
 
-    @pl.loop(0, CHUNKS + STEPS - 1)
-    def _(tick):
-        for step in reversed(range(1, STEPS)):
-            chunk = tick - (step - 1)
-
-            @pl.when(jnp.logical_and(chunk >= 0, chunk < CHUNKS))
-            def _(step=step, chunk=chunk):
-                arrived(step - 1, chunk)
-                start(step, chunk)
-
-        last = tick - (STEPS - 1)
-
-        @pl.when(last == 0)
+    fetch.wait()
+
+    @pl.loop(0, CHUNKS)
+    def _(chunk):
+        @pl.when(chunk == 1)
         def _():
-            fetch.wait()
-
-        @pl.when(last >= 0)
-        def _():
-            arrived(STEPS - 1, last)
-            compute(last)
+            advance(4, CHUNKS - 2)
+            advance(4, CHUNKS - 1)
+
+        complete(chunk)
+        compute(chunk)
 
     for by in range(1, NY):
         draw_copy(by, place["y"]).wait_send()

time: 119 us -> 117 us (0.983)
  Pallas kernels: 115 us -> 113 us
    pallas_call x1, Pallas kernels: 115 us -> 113 us  [exposures(): pl.pallas_call(exposure_kernel, out_shape=(jax.ShapeDtypeStruct((dates, S...]
where the time goes in v4:
time: 117 us
  Pallas kernels  113 us (97%)
  local copies, waits for them, and re-layouts  2.67 us (2%)
  between operations  1.29 us (1%)
    pallas_call x1, Pallas kernels, exposures(): pl.pallas_call(exposure_kernel, out_shape=(jax.ShapeDtypeStruct((dates, S...  113 us
    unnamed x2, local copies, waits for them, and re-layouts  2.67 us

profile of v4, /device:TPU:1, one launch (start us, length us, event | category | flops | bytes accessed | tf_op | source)
XLA Modules:
  0.0 116.7 jit_solution(13614001093059603426)
XLA Ops:
  1.3 112.7 %exposures.1 = (f32[2,16,512]{2,1,0:T(8,128)}, f32[2,16]{1,0:T(2,128)}) custom-call(bf16[2,512,128]{2,1,0:T(8,128)(2,1)} %draws_hbm.1, bf16[128,4096]{1,0:T(8,128)(2,1)} %root_hbm.1, bf16[4096,2048]{1,0:T(8,128)(2,1)} %sens_hbm.1, f32[32,128]{1,0:T(8,128)} %bitcast.8, f32[1,2048]{1,0:T(1,128)} %bitcast.9, f32[1,2048]{1,0:T(1,128)} %bitcast.10, ...), custom_call_target="tpu_custom_call" | custom-call | flops 19327352832 | bytes 17825792 | tf_op jit(solution)/shard_map/exposures/pallas_call | solution.py:540
  114.0 1.5 %copy.13 = f32[2,512,16]{1,2,0:T(8,128)} copy(f32[2,512,16]{1,2,0:T(8,128)} %bitcast.7) | data formatting | bytes 131072
  115.5 1.2 %copy.14 = f32[2,16]{1,0:T(2,128)} copy(f32[2,16]{1,0:T(2,128)} %get-tuple-element.9) | data formatting | bytes 256

commit v5 on v4

--- a/solution.py
+++ b/solution.py
@@ -19,7 +19,8 @@
 PARTS = (
     ((0, 3), (0, 32), ("z", "y", "x")),
     ((0, 3), (32, 32), ("z", "x", "y")),
-    ((3, 1), (0, 64), ("x", "y", "z")),
+    ((3, 1), (0, 32), ("x", "y", "z")),
+    ((3, 1), (32, 32), ("y", "x", "z")),
 )
 STEPS = 5
 DRAW_ORDERS = (("z", "x"), ("x", "z"))
@@ -103,7 +104,7 @@
     draws, root, book, sens, member, weight, net, prices, net_out, net_in, mean_in,
     draw_send, draw_recv, draw_ring_send, draw_ring_recv,
     root_send, root_recv, root_ring_send, root_ring_recv, twin_send, twin_recv,
-    send_sems, recv_sems, own_sems, sens_sem, net_send_sem, net_recv_sems,
+    send_sems, recv_sems, own_sems, sens_sem, net_send_sems, net_recv_sems,
     mean_send, mean_recv,
 ):
     place = trade_place()
@@ -235,11 +236,6 @@
         ref = root.at[from_core, :, (place["y"] + by) % NY]
         return remote(ref, ref, twin_send.at[by], twin_recv.at[by], scen=twin)
 
-    weight[...] = jnp.where(
-        lax.broadcasted_iota(jnp.int32, (1, positions), 1) < live_ref[...],
-        principal_ref[...], 0.0,
-    )
-
     own_draws.wait()
     for by in range(1, NY):
         draw_copy(by, (place["y"] + NY - by) % NY).wait_recv()
@@ -278,10 +274,7 @@
     for part in range(HALVES):
         draw_advance(1, part)
 
-    for copy in root_ring(0, "recv"):
-        copy.wait_recv()
-    for copy in root_ring(1, "send"):
-        copy.start()
+    hand_on(root_ring(0, "recv"), root_ring(1, "send"), True)
     twin_copy(1, core).start()
     twin_copy(3, core).start()
 
@@ -291,12 +284,6 @@
     for copy in root_ring(1, "recv"):
         copy.wait_recv()
     twin_copy(2, core).start()
-
-    @pl.loop(0, positions // TILE)
-    def _(tile):
-        at = pl.ds(pl.multiple_of(tile * TILE, TILE), TILE)
-        labels = lax.broadcasted_iota(jnp.int32, (sets, TILE), 0)
-        member[:, at] = (labels == group_ref[:, at]).astype(F32).astype(BF16)
 
     for by in range(NY):
         twin_copy(by, 1 - core).wait_recv()
@@ -396,11 +383,33 @@
         advance(4, chunk)
         advance(3, chunk + 2)
 
-    def net_copy(chunk, target):
+    def net_copy(late, target):
+        first, count = ((0, CHUNKS - 1), (CHUNKS - 1, 1))[late]
         return remote(
-            net_out.at[chunk, target], net_in.at[chunk, me],
-            net_send_sem, net_recv_sems.at[chunk], trade=target,
-        )
+            net_out.at[target, pl.ds(first, count)], net_in.at[me, pl.ds(first, count)],
+            net_send_sems.at[late], net_recv_sems.at[late], trade=target,
+        )
+
+    def send_nets(late):
+        @pl.loop(1, N_TRADE)
+        def _(step):
+            net_copy(late, (me + step) % N_TRADE).start()
+
+    def await_nets(late):
+        first, count = ((0, CHUNKS - 1), (CHUNKS - 1, 1))[late]
+        whole = remote(
+            net_out.at[pl.ds(0, N_TRADE - 1), pl.ds(first, count)],
+            net_in.at[pl.ds(0, N_TRADE - 1), pl.ds(first, count)],
+            net_send_sems.at[late], net_recv_sems.at[late], trade=me,
+        )
+        whole.wait_send()
+        whole.wait_recv()
+
+    def add_nets(chunk):
+        total = jnp.zeros((SETS_DEV, NY * ROWS), F32)
+        for sender in range(N_TRADE):
+            total = total + net_in[sender, chunk].astype(F32)
+        net[pl.ds(pl.multiple_of(chunk * SETS_DEV, SETS_DEV), SETS_DEV), :] = jnp.maximum(total, 0.0)
 
     def compute(chunk):
         net[...] = jnp.zeros_like(net)
@@ -440,13 +449,20 @@
         settle(tiles - 2, 0)
         settle(tiles - 1, 1)
 
-        net_out[chunk] = net[...].astype(BF16).reshape(N_TRADE, SETS_DEV, NY * ROWS)
-
-        @pl.loop(1, N_TRADE)
-        def _(step):
-            net_copy(chunk, (me + step) % N_TRADE).start()
-
-        net_in[chunk, me] = net_out[chunk, me]
+        for owner in range(N_TRADE):
+            net_out[owner, chunk] = net[owner * SETS_DEV:(owner + 1) * SETS_DEV].astype(BF16)
+        net_in[me, chunk] = net_out[me, chunk]
+
+    weight[...] = jnp.where(
+        lax.broadcasted_iota(jnp.int32, (1, positions), 1) < live_ref[...],
+        principal_ref[...], 0.0,
+    )
+
+    @pl.loop(0, positions // TILE)
+    def _(tile):
+        at = pl.ds(pl.multiple_of(tile * TILE, TILE), TILE)
+        labels = lax.broadcasted_iota(jnp.int32, (sets, TILE), 0)
+        member[:, at] = (labels == group_ref[:, at]).astype(F32).astype(BF16)
 
     fetch.wait()
 
@@ -458,7 +474,14 @@
             advance(4, CHUNKS - 1)
 
         complete(chunk)
+
+        @pl.when(chunk == CHUNKS - 1)
+        def _():
+            send_nets(0)
+
         compute(chunk)
+
+    send_nets(1)
 
     for by in range(1, NY):
         draw_copy(by, place["y"]).wait_send()
@@ -485,18 +508,14 @@
                 for copy in descriptors(part, step, chunk, "send"):
                     copy.wait_send()
 
-    @pl.loop(0, CHUNKS)
+    await_nets(0)
+
+    @pl.loop(0, CHUNKS - 1)
     def _(chunk):
-        whole = remote(
-            net_out.at[chunk, pl.ds(0, N_TRADE - 1)], net_in.at[chunk, pl.ds(0, N_TRADE - 1)],
-            net_send_sem, net_recv_sems.at[chunk], trade=me,
-        )
-        whole.wait_send()
-        whole.wait_recv()
-        total = jnp.zeros((SETS_DEV, NY * ROWS), F32)
-        for sender in range(N_TRADE):
-            total = total + net_in[chunk, sender].astype(F32)
-        net[pl.ds(pl.multiple_of(chunk * SETS_DEV, SETS_DEV), SETS_DEV), :] = jnp.maximum(total, 0.0)
+        add_nets(chunk)
+
+    await_nets(1)
+    add_nets(CHUNKS - 1)
 
     mean_in[scen] = jnp.zeros(mean_in.shape[1:], F32)
     down = lax.broadcasted_iota(jnp.int32, (SETS_DEV, LANES), 0)
@@ -554,15 +573,15 @@
             pltpu.VMEM((1, positions), F32),
             pltpu.VMEM((sets, NY * ROWS), F32),
             pltpu.VMEM((2, NY * ROWS, TILE), F32),
-            pltpu.VMEM((CHUNKS, N_TRADE, SETS_DEV, NY * ROWS), BF16),
-            pltpu.VMEM((CHUNKS, N_TRADE, SETS_DEV, NY * ROWS), BF16),
+            pltpu.VMEM((N_TRADE, CHUNKS, SETS_DEV, NY * ROWS), BF16),
+            pltpu.VMEM((N_TRADE, CHUNKS, SETS_DEV, NY * ROWS), BF16),
             pltpu.VMEM((lax.axis_size("scen"), 8, LANES), F32),
             dma((NY - 1,)), dma((NY - 1,)),
             dma((HALVES, dates, DRAW_STEPS, 2)), dma((HALVES, dates, DRAW_STEPS, 2)),
             dma((2, NZ * NX)), dma((2, NZ * NX)),
             dma((2, 2)), dma((2, 2)), dma((NY,)), dma((NY,)),
             dma((CHUNKS, len(PARTS), STEPS, 2)), dma((CHUNKS, len(PARTS), STEPS, 2)),
-            dma((3,)), dma, dma, dma((CHUNKS,)),
+            dma((3,)), dma, dma((2,)), dma((2,)),
             dma((lax.axis_size("scen") - 1,)), dma((lax.axis_size("scen") - 1,)),
         ],
         compiler_params=pltpu.CompilerParams(

time: 117 us -> 111 us (0.949)
  Pallas kernels: 113 us -> 107 us
    pallas_call x1, Pallas kernels: 113 us -> 107 us  [exposures(): pl.pallas_call(exposure_kernel, out_shape=(jax.ShapeDtypeStruct((dates, S...]
where the time goes in v5:
time: 111 us
  Pallas kernels  107 us (96%)
  local copies, waits for them, and re-layouts  2.67 us (2%)
  between operations  1.29 us (1%)
    pallas_call x1, Pallas kernels, exposures(): pl.pallas_call(exposure_kernel, out_shape=(jax.ShapeDtypeStruct((dates, S...  107 us
    unnamed x2, local copies, waits for them, and re-layouts  2.67 us

profile of v5, /device:TPU:1, one launch (start us, length us, event | category | flops | bytes accessed | tf_op | source)
XLA Modules:
  0.0 111.0 jit_solution(17513584478553801226)
XLA Ops:
  1.3 107.0 %exposures.1 = (f32[2,16,512]{2,1,0:T(8,128)}, f32[2,16]{1,0:T(2,128)}) custom-call(bf16[2,512,128]{2,1,0:T(8,128)(2,1)} %draws_hbm.1, bf16[128,4096]{1,0:T(8,128)(2,1)} %root_hbm.1, bf16[4096,2048]{1,0:T(8,128)(2,1)} %sens_hbm.1, f32[32,128]{1,0:T(8,128)} %bitcast.8, f32[1,2048]{1,0:T(1,128)} %bitcast.9, f32[1,2048]{1,0:T(1,128)} %bitcast.10, ...), custom_call_target="tpu_custom_call" | custom-call | flops 19327352832 | bytes 17825792 | tf_op jit(solution)/shard_map/exposures/pallas_call | solution.py:559
  108.3 1.5 %copy.13 = f32[2,512,16]{1,2,0:T(8,128)} copy(f32[2,512,16]{1,2,0:T(8,128)} %bitcast.7) | data formatting | bytes 131072
  109.8 1.2 %copy.14 = f32[2,16]{1,0:T(2,128)} copy(f32[2,16]{1,0:T(2,128)} %get-tuple-element.9) | data formatting | bytes 256

commit v6 on v5

--- a/solution.py
+++ b/solution.py
@@ -26,6 +26,7 @@
 DRAW_ORDERS = (("z", "x"), ("x", "z"))
 DRAW_STEPS = 3
 SLOTS = 10
+NET_GROUPS = ((0, CHUNKS - 2), (CHUNKS - 2, 1), (CHUNKS - 1, 1))
 
 
 def trade_place():
@@ -220,12 +221,14 @@
         right, left = moved(place, "y", 1), moved(place, "y", 3)
         far = (y + 2) % NY
         half = SLOTS // 2
-        if step == 0:
+        if step < 2:
             at = {"send": (y, y), "recv": (left["y"], right["y"])}[kind]
-            refs = [root.at[core, :, a] for a in at]
         else:
             at = {"send": (left["y"], right["y"]), "recv": (far, far)}[kind]
-            refs = [root.at[core, pl.ds(half * way, half), a] for way, a in enumerate(at)]
+        refs = [
+            root.at[core, pl.ds(half * (way if step != 1 else 1 - way), half), a]
+            for way, a in enumerate(at)
+        ]
         for way, target in enumerate((right, left)):
             yield remote(
                 refs[way], refs[way], root_ring_send.at[step, way], root_ring_recv.at[step, way],
@@ -267,21 +270,24 @@
             @pl.when(jnp.logical_and(source < kinds[kind][1], source != zx))
             def _():
                 root_copy(kind, zx, source).wait_recv()
-    for copy in root_ring(0, "send"):
-        copy.start()
+    for step in range(2):
+        for copy in root_ring(step, "send"):
+            copy.start()
     twin_copy(0, core).start()
 
     for part in range(HALVES):
         draw_advance(1, part)
 
-    hand_on(root_ring(0, "recv"), root_ring(1, "send"), True)
+    hand_on(root_ring(0, "recv"), root_ring(2, "send"), True)
+    for copy in root_ring(1, "recv"):
+        copy.wait_recv()
     twin_copy(1, core).start()
     twin_copy(3, core).start()
 
     for part in range(HALVES):
         draw_advance(2, part)
 
-    for copy in root_ring(1, "recv"):
+    for copy in root_ring(2, "recv"):
         copy.wait_recv()
     twin_copy(2, core).start()
 
@@ -368,15 +374,14 @@
     make_levels(0)
     both(0, start)
     both(0, functools.partial(advance, 1))
+    both(0, functools.partial(advance, 2))
     draw_arrived(2, 1)
     make_levels(1)
     both(1, start)
-    both(0, functools.partial(advance, 2))
+    advance(3, 0)
     both(1, functools.partial(advance, 1))
-    advance(3, 0)
-    advance(2, 2)
     advance(3, 1)
-    advance(2, 3)
+    both(1, functools.partial(advance, 2))
 
     @pl.loop(0, CHUNKS - 2)
     def _(chunk):
@@ -384,7 +389,7 @@
         advance(3, chunk + 2)
 
     def net_copy(late, target):
-        first, count = ((0, CHUNKS - 1), (CHUNKS - 1, 1))[late]
+        first, count = NET_GROUPS[late]
         return remote(
             net_out.at[target, pl.ds(first, count)], net_in.at[me, pl.ds(first, count)],
             net_send_sems.at[late], net_recv_sems.at[late], trade=target,
@@ -396,7 +401,7 @@
             net_copy(late, (me + step) % N_TRADE).start()
 
     def await_nets(late):
-        first, count = ((0, CHUNKS - 1), (CHUNKS - 1, 1))[late]
+        first, count = NET_GROUPS[late]
         whole = remote(
             net_out.at[pl.ds(0, N_TRADE - 1), pl.ds(first, count)],
             net_in.at[pl.ds(0, N_TRADE - 1), pl.ds(first, count)],
@@ -468,20 +473,24 @@
 
     @pl.loop(0, CHUNKS)
     def _(chunk):
-        @pl.when(chunk == 1)
+        @pl.when(chunk == CHUNKS - 3)
         def _():
             advance(4, CHUNKS - 2)
+
+        @pl.when(chunk == CHUNKS - 2)
+        def _():
             advance(4, CHUNKS - 1)
+            send_nets(0)
 
         complete(chunk)
 
         @pl.when(chunk == CHUNKS - 1)
         def _():
-            send_nets(0)
+            send_nets(1)
 
         compute(chunk)
 
-    send_nets(1)
+    send_nets(2)
 
     for by in range(1, NY):
         draw_copy(by, place["y"]).wait_send()
@@ -495,7 +504,7 @@
             @pl.loop(1, NZ * NX)
             def _(step):
                 root_copy(kind, (zx + step) % (NZ * NX), zx).wait_send()
-    for step in range(2):
+    for step in range(3):
         for copy in root_ring(step, "send"):
             copy.wait_send()
     for by in range(NY):
@@ -508,14 +517,12 @@
                 for copy in descriptors(part, step, chunk, "send"):
                     copy.wait_send()
 
-    await_nets(0)
-
-    @pl.loop(0, CHUNKS - 1)
-    def _(chunk):
-        add_nets(chunk)
-
-    await_nets(1)
-    add_nets(CHUNKS - 1)
+    for late, (first, count) in enumerate(NET_GROUPS):
+        await_nets(late)
+
+        @pl.loop(first, first + count)
+        def _(chunk):
+            add_nets(chunk)
 
     mean_in[scen] = jnp.zeros(mean_in.shape[1:], F32)
     down = lax.broadcasted_iota(jnp.int32, (SETS_DEV, LANES), 0)
@@ -579,9 +586,9 @@
             dma((NY - 1,)), dma((NY - 1,)),
             dma((HALVES, dates, DRAW_STEPS, 2)), dma((HALVES, dates, DRAW_STEPS, 2)),
             dma((2, NZ * NX)), dma((2, NZ * NX)),
-            dma((2, 2)), dma((2, 2)), dma((NY,)), dma((NY,)),
+            dma((3, 2)), dma((3, 2)), dma((NY,)), dma((NY,)),
             dma((CHUNKS, len(PARTS), STEPS, 2)), dma((CHUNKS, len(PARTS), STEPS, 2)),
-            dma((3,)), dma, dma((2,)), dma((2,)),
+            dma((3,)), dma, dma((len(NET_GROUPS),)), dma((len(NET_GROUPS),)),
             dma((lax.axis_size("scen") - 1,)), dma((lax.axis_size("scen") - 1,)),
         ],
         compiler_params=pltpu.CompilerParams(

time: 111 us -> 113 us (1.018)
  Pallas kernels: 107 us -> 109 us
    pallas_call x1, Pallas kernels: 107 us -> 109 us  [exposures(): pl.pallas_call(exposure_kernel, out_shape=(jax.ShapeDtypeStruct((dates, S...]
where the time goes in v6:
time: 113 us
  Pallas kernels  109 us (96%)
  local copies, waits for them, and re-layouts  2.67 us (2%)
  between operations  1.29 us (1%)
    pallas_call x1, Pallas kernels, exposures(): pl.pallas_call(exposure_kernel, out_shape=(jax.ShapeDtypeStruct((dates, S...  109 us
    unnamed x2, local copies, waits for them, and re-layouts  2.67 us

profile of v6, /device:TPU:1, one launch (start us, length us, event | category | flops | bytes accessed | tf_op | source)
XLA Modules:
  0.0 112.7 jit_solution(720007136802978076)
XLA Ops:
  1.3 108.7 %exposures.1 = (f32[2,16,512]{2,1,0:T(8,128)}, f32[2,16]{1,0:T(2,128)}) custom-call(bf16[2,512,128]{2,1,0:T(8,128)(2,1)} %draws_hbm.1, bf16[128,4096]{1,0:T(8,128)(2,1)} %root_hbm.1, bf16[4096,2048]{1,0:T(8,128)(2,1)} %sens_hbm.1, f32[32,128]{1,0:T(8,128)} %bitcast.8, f32[1,2048]{1,0:T(1,128)} %bitcast.9, f32[1,2048]{1,0:T(1,128)} %bitcast.10, ...), custom_call_target="tpu_custom_call" | custom-call | flops 19327352832 | bytes 17825792 | tf_op jit(solution)/shard_map/exposures/pallas_call | solution.py:566
  110.0 1.5 %copy.13 = f32[2,512,16]{1,2,0:T(8,128)} copy(f32[2,512,16]{1,2,0:T(8,128)} %bitcast.7) | data formatting | bytes 131072
  111.5 1.2 %copy.14 = f32[2,16]{1,0:T(2,128)} copy(f32[2,16]{1,0:T(2,128)} %get-tuple-element.9) | data formatting | bytes 256

commit v7 on v6

--- a/solution.py
+++ b/solution.py
@@ -26,7 +26,7 @@
 DRAW_ORDERS = (("z", "x"), ("x", "z"))
 DRAW_STEPS = 3
 SLOTS = 10
-NET_GROUPS = ((0, CHUNKS - 2), (CHUNKS - 2, 1), (CHUNKS - 1, 1))
+NET_GROUPS = ((0, CHUNKS - 1), (CHUNKS - 1, 1))
 
 
 def trade_place():
@@ -127,10 +127,9 @@
 
     barrier = pltpu.get_barrier_semaphore()
 
-    @pl.loop(1, N_TRADE)
-    def _(step):
+    for step in range(1, N_TRADE):
         pl.semaphore_signal(
-            barrier, inc=1, device_id={"trade": (me + step) % N_TRADE},
+            barrier, inc=1, device_id={"trade": lax.rem(me + step, N_TRADE)},
             device_id_type=pl.DeviceIdType.MESH,
         )
 
@@ -374,14 +373,15 @@
     make_levels(0)
     both(0, start)
     both(0, functools.partial(advance, 1))
-    both(0, functools.partial(advance, 2))
     draw_arrived(2, 1)
     make_levels(1)
     both(1, start)
+    both(0, functools.partial(advance, 2))
+    both(1, functools.partial(advance, 1))
     advance(3, 0)
-    both(1, functools.partial(advance, 1))
+    advance(2, 2)
     advance(3, 1)
-    both(1, functools.partial(advance, 2))
+    advance(2, 3)
 
     @pl.loop(0, CHUNKS - 2)
     def _(chunk):
@@ -396,9 +396,8 @@
         )
 
     def send_nets(late):
-        @pl.loop(1, N_TRADE)
-        def _(step):
-            net_copy(late, (me + step) % N_TRADE).start()
+        for step in range(1, N_TRADE):
+            net_copy(late, lax.rem(me + step, N_TRADE)).start()
 
     def await_nets(late):
         first, count = NET_GROUPS[late]
@@ -447,6 +446,11 @@
         def _(pair):
             price(2 * pair + 1, 1)
             settle(2 * pair, 0)
+
+            @pl.when(chunk < CHUNKS - 2)
+            def _():
+                advance(4, chunk + 2)
+
             price(2 * pair + 2, 0)
             settle(2 * pair + 1, 1)
 
@@ -473,24 +477,15 @@
 
     @pl.loop(0, CHUNKS)
     def _(chunk):
-        @pl.when(chunk == CHUNKS - 3)
-        def _():
-            advance(4, CHUNKS - 2)
-
-        @pl.when(chunk == CHUNKS - 2)
-        def _():
-            advance(4, CHUNKS - 1)
-            send_nets(0)
-
         complete(chunk)
 
         @pl.when(chunk == CHUNKS - 1)
         def _():
-            send_nets(1)
+            send_nets(0)
 
         compute(chunk)
 
-    send_nets(2)
+    send_nets(1)
 
     for by in range(1, NY):
         draw_copy(by, place["y"]).wait_send()

time: 113 us -> 108 us (0.956)
  Pallas kernels: 109 us -> 104 us
    pallas_call x1, Pallas kernels: 109 us -> 104 us  [exposures(): pl.pallas_call(exposure_kernel, out_shape=(jax.ShapeDtypeStruct((dates, S...]
where the time goes in v7:
time: 108 us
  Pallas kernels  104 us (96%)
  local copies, waits for them, and re-layouts  2.67 us (2%)
  between operations  1.29 us (1%)
    pallas_call x1, Pallas kernels, exposures(): pl.pallas_call(exposure_kernel, out_shape=(jax.ShapeDtypeStruct((dates, S...  104 us
    unnamed x2, local copies, waits for them, and re-layouts  2.67 us

profile of v7, /device:TPU:1, one launch (start us, length us, event | category | flops | bytes accessed | tf_op | source)
XLA Modules:
  0.0 108.3 jit_solution(12840013122537924348)
XLA Ops:
  1.3 104.3 %exposures.1 = (f32[2,16,512]{2,1,0:T(8,128)}, f32[2,16]{1,0:T(2,128)}) custom-call(bf16[2,512,128]{2,1,0:T(8,128)(2,1)} %draws_hbm.1, bf16[128,4096]{1,0:T(8,128)(2,1)} %root_hbm.1, bf16[4096,2048]{1,0:T(8,128)(2,1)} %sens_hbm.1, f32[32,128]{1,0:T(8,128)} %bitcast.8, f32[1,2048]{1,0:T(1,128)} %bitcast.9, f32[1,2048]{1,0:T(1,128)} %bitcast.10, ...), custom_call_target="tpu_custom_call" | custom-call | flops 19327352832 | bytes 17825792 | tf_op jit(solution)/shard_map/exposures/pallas_call | solution.py:561
  105.6 1.5 %copy.13 = f32[2,512,16]{1,2,0:T(8,128)} copy(f32[2,512,16]{1,2,0:T(8,128)} %bitcast.7) | data formatting | bytes 131072
  107.1 1.2 %copy.14 = f32[2,16]{1,0:T(2,128)} copy(f32[2,16]{1,0:T(2,128)} %get-tuple-element.9) | data formatting | bytes 256

commit v8 on v7

--- a/solution.py
+++ b/solution.py
@@ -127,10 +127,11 @@
 
     barrier = pltpu.get_barrier_semaphore()
 
-    for step in range(1, N_TRADE):
+    greeted = [trade_index(moved(place, "y", by)) for by in range(1, NY)]
+    greeted += [lax.rem(me + step * NY, N_TRADE) for step in range(1, NZ * NX)]
+    for target in greeted:
         pl.semaphore_signal(
-            barrier, inc=1, device_id={"trade": lax.rem(me + step, N_TRADE)},
-            device_id_type=pl.DeviceIdType.MESH,
+            barrier, inc=1, device_id={"trade": target}, device_id_type=pl.DeviceIdType.MESH,
         )
 
     @pl.loop(1, scens)
@@ -140,7 +141,7 @@
             device_id_type=pl.DeviceIdType.MESH,
         )
 
-    pl.semaphore_wait(barrier, N_TRADE - 1 + scens - 1)
+    pl.semaphore_wait(barrier, len(greeted) + scens - 1)
 
     def draw_rows(y):
         return draws_hbm.at[:, pl.ds(y * span, span), :]
@@ -473,20 +474,6 @@
         labels = lax.broadcasted_iota(jnp.int32, (sets, TILE), 0)
         member[:, at] = (labels == group_ref[:, at]).astype(F32).astype(BF16)
 
-    fetch.wait()
-
-    @pl.loop(0, CHUNKS)
-    def _(chunk):
-        complete(chunk)
-
-        @pl.when(chunk == CHUNKS - 1)
-        def _():
-            send_nets(0)
-
-        compute(chunk)
-
-    send_nets(1)
-
     for by in range(1, NY):
         draw_copy(by, place["y"]).wait_send()
     for part in range(HALVES):
@@ -505,12 +492,33 @@
     for by in range(NY):
         twin_copy(by, core).wait_send()
 
+    def sent(first, last, chunk):
+        for part in range(len(PARTS)):
+            for step in range(first, last):
+                for copy in descriptors(part, step, chunk, "send"):
+                    copy.wait_send()
+
     @pl.loop(0, CHUNKS)
     def _(chunk):
-        for part in range(len(PARTS)):
-            for step in range(STEPS):
-                for copy in descriptors(part, step, chunk, "send"):
-                    copy.wait_send()
+        sent(0, 3, chunk)
+
+    fetch.wait()
+
+    @pl.loop(0, CHUNKS)
+    def _(chunk):
+        complete(chunk)
+
+        @pl.when(chunk == CHUNKS - 1)
+        def _():
+            send_nets(0)
+
+        compute(chunk)
+
+    send_nets(1)
+
+    @pl.loop(0, CHUNKS)
+    def _(chunk):
+        sent(3, STEPS, chunk)
 
     for late, (first, count) in enumerate(NET_GROUPS):
         await_nets(late)

time: 108 us -> 107 us (level)
    pallas_call x1, Pallas kernels: 104 us -> 103 us  [exposures(): pl.pallas_call(exposure_kernel, out_shape=(jax.ShapeDtypeStruct((dates, S...]
where the time goes in v8:
time: 107 us
  Pallas kernels  103 us (96%)
  local copies, waits for them, and re-layouts  2.67 us (2%)
  between operations  1.29 us (1%)
    pallas_call x1, Pallas kernels, exposures(): pl.pallas_call(exposure_kernel, out_shape=(jax.ShapeDtypeStruct((dates, S...  103 us
    unnamed x2, local copies, waits for them, and re-layouts  2.67 us

profile of v8, /device:TPU:1, one launch (start us, length us, event | category | flops | bytes accessed | tf_op | source)
XLA Modules:
  0.0 107.0 jit_solution(8226810342685016396)
XLA Ops:
  1.3 103.0 %exposures.1 = (f32[2,16,512]{2,1,0:T(8,128)}, f32[2,16]{1,0:T(2,128)}) custom-call(bf16[2,512,128]{2,1,0:T(8,128)(2,1)} %draws_hbm.1, bf16[128,4096]{1,0:T(8,128)(2,1)} %root_hbm.1, bf16[4096,2048]{1,0:T(8,128)(2,1)} %sens_hbm.1, f32[32,128]{1,0:T(8,128)} %bitcast.8, f32[1,2048]{1,0:T(1,128)} %bitcast.9, f32[1,2048]{1,0:T(1,128)} %bitcast.10, ...), custom_call_target="tpu_custom_call" | custom-call | flops 19327352832 | bytes 17825792 | tf_op jit(solution)/shard_map/exposures/pallas_call | solution.py:569
  104.3 1.5 %copy.13 = f32[2,512,16]{1,2,0:T(8,128)} copy(f32[2,512,16]{1,2,0:T(8,128)} %bitcast.7) | data formatting | bytes 131072
  105.8 1.2 %copy.14 = f32[2,16]{1,0:T(2,128)} copy(f32[2,16]{1,0:T(2,128)} %get-tuple-element.9) | data formatting | bytes 256

commit v9 on v8

--- a/solution.py
+++ b/solution.py
@@ -414,7 +414,7 @@
         total = jnp.zeros((SETS_DEV, NY * ROWS), F32)
         for sender in range(N_TRADE):
             total = total + net_in[sender, chunk].astype(F32)
-        net[pl.ds(pl.multiple_of(chunk * SETS_DEV, SETS_DEV), SETS_DEV), :] = jnp.maximum(total, 0.0)
+        net[pl.ds(pl.multiple_of(chunk * SETS_DEV, SETS_DEV), SETS_DEV), :] = total
 
     def compute(chunk):
         net[...] = jnp.zeros_like(net)
@@ -539,6 +539,7 @@
             axis=1,
         )
         out_ref[date] = strip
+        strip = jnp.maximum(strip, 0.0)
         sums = jnp.where(down == across, jnp.sum(strip, axis=1, keepdims=True), 0.0)
         mean_in[scen, pl.ds(date, 1), :] = jnp.sum(sums, axis=0, keepdims=True)
 
@@ -554,7 +555,7 @@
     for by in range(1, scens):
         mean_copy(by, (scen + scens - by) % scens).wait_recv()
         mean_copy(by, scen).wait_send()
-    total = jnp.sum(mean_in[...], axis=0) / (scens * NY * span)
+    total = jnp.sum(mean_in[...], axis=0)
     mean_ref[...] = total[:dates, :SETS_DEV]
 
 
@@ -611,11 +612,12 @@
     normal_draws, covariance_root, mean_pullback, sensitivity_tensor,
     moneyness_shift, signed_principal, deal_agreement_group, active_position_number,
 ):
-    exposure, mean = exposures(
+    nets, sums = exposures(
         normal_draws, covariance_root, sensitivity_tensor, mean_pullback, moneyness_shift,
         signed_principal, deal_agreement_group, active_position_number,
     )
-    return exposure.transpose(0, 2, 1), mean
+    exposure = jnp.maximum(nets, 0.0).transpose(0, 2, 1)
+    return exposure, sums / (normal_draws.shape[1] * lax.axis_size("scen"))
 
 
 def solution(mesh):

time: 107 us -> 107 us (level)
  other arithmetic: 0 us -> 2.67 us
  local copies, waits for them, and re-layouts: 2.67 us -> 0 us
    unnamed x2 -> x0, local copies, waits for them, and re-layouts: 2.67 us -> none
    transpose x0 -> x1, other arithmetic: none -> 1.48 us  [on_device(): exposure = jnp.maximum(nets, 0.0).transpose(0, 2, 1)]
    div x0 -> x1, other arithmetic: none -> 1.2 us  [on_device(): return (exposure, sums / (normal_draws.shape[1] * lax.axis_size('scen')))]
where the time goes in v9:
time: 107 us
  Pallas kernels  103 us (96%)
  other arithmetic  2.67 us (2%)
  between operations  1.29 us (1%)
    pallas_call x1, Pallas kernels, exposures(): pl.pallas_call(exposure_kernel, out_shape=(jax.ShapeDtypeStruct((dates, S...  103 us

profile of v9, /device:TPU:1, one launch (start us, length us, event | category | flops | bytes accessed | tf_op | source)
XLA Modules:
  0.0 107.0 jit_solution(12824097187122954414)
XLA Ops:
  1.3 103.0 %exposures.1 = (f32[2,16,512]{2,1,0:T(8,128)}, f32[2,16]{1,0:T(2,128)}) custom-call(bf16[2,512,128]{2,1,0:T(8,128)(2,1)} %draws_hbm.1, bf16[128,4096]{1,0:T(8,128)(2,1)} %root_hbm.1, bf16[4096,2048]{1,0:T(8,128)(2,1)} %sens_hbm.1, f32[32,128]{1,0:T(8,128)} %bitcast.8, f32[1,2048]{1,0:T(1,128)} %bitcast.9, f32[1,2048]{1,0:T(1,128)} %bitcast.10, ...), custom_call_target="tpu_custom_call" | custom-call | flops 19327352832 | bytes 17825792 | tf_op jit(solution)/shard_map/exposures/pallas_call | solution.py:570
  104.3 1.5 %maximum_bitcast_fusion = f32[2,512,16]{1,2,0:T(8,128)} fusion(f32[2,16,512]{2,1,0:T(8,128)} %get-tuple-element.4), kind=kLoop, calls=%fused_computation | loop fusion | flops 16384 | bytes 131072 | tf_op jit(solution)/shard_map/transpose | solution.py:619
  105.8 1.2 %broadcast_multiply_fusion = f32[2,16]{1,0:T(2,128)} fusion(f32[2,16]{1,0:T(2,128)} %get-tuple-element.5), kind=kLoop, calls=%fused_computation.1 | loop fusion | flops 32 | bytes 256 | tf_op jit(solution)/shard_map/div | solution.py:620
